TPU v7x, 128 devices: a whole 4x4x4 slice. The times are simulated.
128 devices in a mesh: section: 4 (over z), expert: 32 (over x, y, core).
Axes of the slice: x: 4, y: 4, z: 4, core: 2. Of those that a mesh axis runs over, the one named last changes fastest.
Arguments:
- tokens: bfloat16 [4096, 4096], P('expert'), may hold values from -6 to 6
- cotangent: bfloat16 [4096, 4096], P('expert'), may hold values from -6 to 6
- w_down: bfloat16 [4, 4096, 512], P('section', 'expert'), may hold values from -0.09375 to 0.09375
- w_up: bfloat16 [4, 512, 4096], P('section', 'expert'), may hold values from -0.25 to 0.25
- w_gate_up: bfloat16 [4, 32, 512, 2048], P('section', 'expert'), may hold values from -0.25 to 0.25
- w_out: bfloat16 [4, 32, 1024, 512], P('section', 'expert'), may hold values from -0.1875 to 0.1875
- routes: int32 [4, 4096, 2], P('section', 'expert'), may hold values from 0 to 31, all different within a row; in each aligned block of 128 rows (0 to 127, 128 to 255, ..., all dimensions but the last counted through in order) at most 12 rows name the same one
- gates: float32 [4, 4096, 2], P('section', 'expert'), may hold values from 0.3 to 1
- token_counts: int32 [4, 32], P('section', 'expert'), may hold values from 96 to 128, as said below
Outputs:
- layer_outputs: bfloat16 [4, 4096, 4096], P('section', 'expert')
- input_grads: bfloat16 [4, 4096, 4096], P('section', 'expert')
Inputs may be any that keep to these rules, and one draw needn't show every extreme that they name: `routes`: A token's 2 experts differ. In each aligned block of 128 rows of a layer no expert is named by more than 12 rows. `token_counts`: in every layer some block has all 128 tokens live.
All inputs are finite; a program needn't handle non-finite values.
Results may differ from a plain program's by a relative error of at most 0.04.
Values may be sent and summed in bfloat16 or wider, within the bound.
A program may use at most 128 MiB of HBM per device.

v0:
```python
import jax
import jax.numpy as jnp
from jax import lax
from jax.sharding import PartitionSpec as P

EPS = 1e-05


def shifted(block, axis, distance):
    devices = range(lax.axis_size(axis))
    route = [(i - distance, i) for i in devices if i - distance in devices]
    return lax.ppermute(block, axis, route)


def route_slots(route_ids, count, experts, capacity):
    tokens_here, fanout = route_ids.shape
    live = jnp.broadcast_to(
        (jnp.arange(tokens_here, dtype=jnp.int32) < count)[:, None], (tokens_here, fanout)
    ).reshape(-1)
    flat_ids = route_ids.reshape(-1)
    onehot = (
        (flat_ids[:, None] == jnp.arange(experts, dtype=jnp.int32)[None, :]) & live[:, None]
    ).astype(jnp.int32)
    before = jnp.cumsum(onehot, axis=0, dtype=jnp.int32) - onehot
    slot = jnp.sum(before * onehot, axis=1, dtype=jnp.int32)
    dest = jnp.where(live, flat_ids * capacity + slot, experts * capacity)
    loads = jnp.sum(onehot, axis=0, dtype=jnp.int32)
    return (dest, live, loads)


def expert_forward(rows, w_gate_up, w_out):
    width = w_out.shape[0]
    both = jnp.dot(rows, w_gate_up, preferred_element_type=jnp.float32)
    hidden = (jax.nn.silu(both[:, :width]) * both[:, width:]).astype(jnp.bfloat16)
    return jnp.dot(hidden, w_out, preferred_element_type=jnp.float32).astype(jnp.bfloat16)


def expert_backward(rows, grads, w_gate_up, w_out):
    width = w_out.shape[0]
    both = jnp.dot(rows, w_gate_up, preferred_element_type=jnp.float32)
    gate_part = both[:, :width]
    up_part = both[:, width:]
    sigma = jax.nn.sigmoid(gate_part)
    hidden_grad = lax.dot_general(
        grads, w_out, (((1,), (1,)), ((), ())), preferred_element_type=jnp.float32
    )
    gate_grad = hidden_grad * up_part * sigma * (1.0 + gate_part * (1.0 - sigma))
    up_grad = hidden_grad * gate_part * sigma
    joined = jnp.concatenate([gate_grad, up_grad], axis=1).astype(jnp.bfloat16)
    return lax.dot_general(
        joined, w_gate_up, (((1,), (1,)), ((), ())), preferred_element_type=jnp.float32
    ).astype(jnp.bfloat16)


def normalize(inputs):
    values = inputs.astype(jnp.float32)
    inv_rms = lax.rsqrt(jnp.mean(values * values, axis=1, keepdims=True) + EPS)
    return (values, inv_rms)


def body(tokens, cotangent, w_down, w_up, w_gate_up, w_out, routes, gates, token_counts):
    sections = lax.axis_size("section")
    here = lax.axis_index("section")
    experts = lax.axis_size("expert")
    tokens_here = tokens.shape[0]
    fanout = routes.shape[2]
    capacity = 3 * tokens_here * fanout // (2 * experts)
    slots = experts * capacity
    down_full, up_full = (
        lax.all_gather(w_down, "expert", axis=1, tiled=True),
        lax.all_gather(w_up, "expert", axis=1, tiled=True),
    )
    proj_down = down_full[0]
    proj_up = up_full[0]
    latent_width = proj_down.shape[1]
    expert_in = w_gate_up[0, 0]
    expert_back = w_out[0, 0]
    dest, live, loads = route_slots(routes[0], token_counts[0, 0], experts, capacity)
    safe_dest = jnp.minimum(dest, slots - 1)
    live_pairs = live.reshape(tokens_here, fanout).astype(jnp.float32)
    weights = gates[0] * live_pairs
    load_column = loads.reshape(experts, 1)
    empty_send = jnp.zeros((experts, capacity, latent_width), jnp.bfloat16)
    empty_latent = jnp.zeros((tokens_here, latent_width), jnp.bfloat16)
    empty_rows = jnp.zeros((slots, latent_width), jnp.bfloat16)
    empty_loads = jnp.zeros((experts, 1), jnp.int32)

    def scatter_rows(values):
        placed = jnp.zeros((slots, latent_width), jnp.bfloat16).at[dest].set(values, mode="drop")
        return placed.reshape(experts, capacity, latent_width)

    def combine(returned, scale):
        picked = jnp.take(returned.reshape(slots, latent_width), safe_dest, axis=0)
        picked = picked.astype(jnp.float32).reshape(tokens_here, fanout, latent_width)
        return jnp.sum(scale[:, :, None] * picked, axis=1)

    def forward_rows(part):
        return expert_forward(part, expert_in, expert_back)

    def backward_rows(part, grads):
        return expert_backward(part, grads, expert_in, expert_back)

    def run_experts(operands):
        rows, arrived = operands
        return forward_rows(rows)

    def grad_experts(operands):
        rows, grads, arrived = operands
        return backward_rows(rows, grads)

    def skip_rows(operands):
        return empty_rows

    def forward_prepare(inputs):
        values, inv_rms = normalize(inputs)
        normed = (values * inv_rms).astype(jnp.bfloat16)
        latent = jnp.dot(normed, proj_down, preferred_element_type=jnp.float32).astype(jnp.bfloat16)
        return (scatter_rows(jnp.repeat(latent, fanout, axis=0)), latent, load_column)

    def skip_prepare(inputs):
        return (empty_send, empty_latent, empty_loads)

    def forward_finish(operands):
        inputs, returned = operands
        values = inputs.astype(jnp.float32)
        mixed = combine(returned, weights).astype(jnp.bfloat16)
        return (values + jnp.dot(mixed, proj_up, preferred_element_type=jnp.float32)).astype(
            jnp.bfloat16
        )

    def skip_finish(operands):
        return jnp.zeros_like(operands[0])

    def backward_prepare(operands):
        grad, latent = operands
        mix_grad = lax.dot_general(
            grad, proj_up, (((1,), (1,)), ((), ())), preferred_element_type=jnp.float32
        ).astype(jnp.bfloat16)
        route_grad = (weights[:, :, None] * mix_grad[:, None, :].astype(jnp.float32)).astype(
            jnp.bfloat16
        )
        send = scatter_rows(route_grad.reshape(-1, latent_width))
        again = scatter_rows(jnp.repeat(latent, fanout, axis=0))
        return (send, again, load_column)

    def skip_backward_prepare(operands):
        return (empty_send, empty_send, empty_loads)

    def backward_finish(operands):
        inputs, grad, returned = operands
        values, inv_rms = normalize(inputs)
        latent_grad = combine(returned, live_pairs).astype(jnp.bfloat16)
        normed_grad = lax.dot_general(
            latent_grad, proj_down, (((1,), (1,)), ((), ())), preferred_element_type=jnp.float32
        )
        unit = values * inv_rms
        dotted = jnp.mean(normed_grad * unit, axis=1, keepdims=True)
        return (grad.astype(jnp.float32) + inv_rms * (normed_grad - unit * dotted)).astype(
            jnp.bfloat16
        )

    def skip_backward_finish(operands):
        return jnp.zeros_like(operands[0])

    current = tokens
    layer_in = jnp.zeros_like(tokens)
    layer_out = jnp.zeros_like(tokens)
    kept_rows = empty_rows
    kept_loads = empty_loads
    kept_latent = empty_latent
    for step in range(sections):
        mine = here == step
        send, latent, counts_out = lax.cond(mine, forward_prepare, skip_prepare, current)
        arrived_rows, arrived = (
            lax.all_to_all(send, "expert", split_axis=0, concat_axis=0, tiled=True),
            lax.all_to_all(counts_out, "expert", split_axis=0, concat_axis=0, tiled=True),
        )
        rows = arrived_rows.reshape(slots, latent_width)
        outcome = lax.cond(mine, run_experts, skip_rows, (rows, arrived))
        returned = lax.all_to_all(
            outcome.reshape(experts, capacity, latent_width),
            "expert",
            split_axis=0,
            concat_axis=0,
            tiled=True,
        )
        result = lax.cond(mine, forward_finish, skip_finish, (current, returned))
        layer_in = jnp.where(mine, current, layer_in)
        layer_out = jnp.where(mine, result, layer_out)
        kept_rows = jnp.where(mine, rows, kept_rows)
        kept_loads = jnp.where(mine, arrived, kept_loads)
        kept_latent = jnp.where(mine, latent, kept_latent)
        if step + 1 < sections:
            current = shifted(result, "section", 1)
    grad = cotangent
    input_grad = jnp.zeros_like(tokens)
    for step in reversed(range(sections)):
        mine = here == step
        send, again, counts_out = lax.cond(
            mine, backward_prepare, skip_backward_prepare, (grad, kept_latent)
        )
        grad_rows = lax.all_to_all(send, "expert", split_axis=0, concat_axis=0, tiled=True).reshape(
            slots, latent_width
        )
        rows = kept_rows
        arrived = kept_loads
        lat_rows = lax.cond(mine, grad_experts, skip_rows, (rows, grad_rows, arrived))
        returned = lax.all_to_all(
            lat_rows.reshape(experts, capacity, latent_width),
            "expert",
            split_axis=0,
            concat_axis=0,
            tiled=True,
        )
        result = lax.cond(mine, backward_finish, skip_backward_finish, (layer_in, grad, returned))
        input_grad = jnp.where(mine, result, input_grad)
        if step > 0:
            grad = shifted(result, "section", -1)
    return (layer_out[None], input_grad[None])


def solution(mesh):
    in_specs = (
        P("expert", None),
        P("expert", None),
        P("section", "expert", None),
        P("section", "expert", None),
        P("section", "expert", None, None),
        P("section", "expert", None, None),
        P("section", "expert", None),
        P("section", "expert", None),
        P("section", "expert"),
    )
    out_specs = (P("section", "expert", None), P("section", "expert", None))
    return jax.shard_map(body, mesh=mesh, in_specs=in_specs, out_specs=out_specs, check_vma=False)
```

profile of v0, /device:TPU:1, one launch (start us, length us, event | category | flops | bytes accessed | tf_op | source)
XLA Modules:
  0.0 691.1 jit_solution(9736590388715094300)
XLA Ops:
  11.8 48.0 %all-gather.3.cloned.1.call-done = bf16[1,4096,512]{2,1,0:T(8,128)(2,1)} async-done(((bf16[1,128,512]{2,1,0:T(8,128)(2,1)}), bf16[1,4096,512]{2,1,0:T(8,128)(2,1)}) %all-gather.3.cloned.1.call-update) | async-done | bytes 4194320 | tf_op jit(solution)/shard_map/all_gather | solution.py:70
  59.9 7.7 %conditional.24 = (bf16[32,12,512]{2,1,0:T(8,128)(2,1)}) conditional(s32[]{:T(128)} %convert_element_type.258, () %tuple.158, (s32[256]{0:T(256)S(1)}, bf16[128,4096]{1,0:T(8,128)(2,1)}, bf16[4096,512]{1,0:T(8,128)(2,1)}) %tuple.267), branch_computations={%region_3.4_spmd, %region_4.0_spmd} | conditional | flops 540083072 | bytes 8523786 | solution.py:173
  67.6 5.3 all-to-all-start
  72.9 12.8 %all-to-all-done = bf16[32,12,512]{2,1,0:T(8,128)(2,1)S(1)} async-done(((bf16[32,12,512]{2,1,0:T(8,128)(2,1)}), bf16[32,12,512]{2,1,0:T(8,128)(2,1)S(1)}, u32[]{:S(2)}, u32[]{:S(2)}) %all-to-all-start) | async-done | bytes 393248 | tf_op jit(solution)/shard_map/all_to_all | solution.py:175
  95.3 17.1 %all-gather.5.cloned.1.call-done = bf16[1,512,4096]{2,1,0:T(8,128)(2,1)} async-done(((bf16[1,16,4096]{2,1,0:T(8,128)(2,1)}), bf16[1,512,4096]{2,1,0:T(8,128)(2,1)}) %all-gather.5.cloned.1.call-update) | async-done | bytes 4194320 | tf_op jit(solution)/shard_map/all_gather | solution.py:71
  112.4 12.7 %conditional.26 = (bf16[128,4096]{1,0:T(8,128)(2,1)}) conditional(s32[]{:T(128)} %convert_element_type.258, () %tuple.156, (bf16[128,4096]{1,0:T(8,128)(2,1)S(1)}, f32[128,2]{1,0:T(8,128)}, bf16[32,12,512]{2,1,0:T(8,128)(2,1)}, s32[256]{0:T(256)S(1)}, bf16[512,4096]{1,0:T(8,128)(2,1)}) %tuple.291), branch_computations={%region_9.10_spmd, %region_10.13_spmd} | conditional | flops 538905856 | bytes 10234376 | solution.py:187
  126.5 22.8 %collective-permute-done = bf16[128,4096]{1,0:T(8,128)(2,1)S(1)} collective-permute-done((bf16[128,4096]{1,0:T(8,128)(2,1)}, bf16[128,4096]{1,0:T(8,128)(2,1)S(1)}, u32[]{:S(2)}, u32[]{:S(2)}) %collective-permute-start) | collective-permute-done | bytes 1048608 | tf_op jit(solution)/shard_map/ppermute | solution.py:12
  150.2 5.2 all-to-all-start.2
  155.5 11.7 %all-to-all-done.2 = bf16[32,12,512]{2,1,0:T(8,128)(2,1)} async-done(((bf16[32,12,512]{2,1,0:T(8,128)(2,1)}), bf16[32,12,512]{2,1,0:T(8,128)(2,1)}, u32[]{:S(2)}, u32[]{:S(2)}) %all-to-all-start.2) | async-done | bytes 393248 | tf_op jit(solution)/shard_map/all_to_all | solution.py:175
  174.9 11.4 %all-to-all-done.3 = bf16[32,12,512]{2,1,0:T(8,128)(2,1)} async-done(((bf16[32,12,512]{2,1,0:T(8,128)(2,1)}), bf16[32,12,512]{2,1,0:T(8,128)(2,1)}, u32[]{:S(2)}, u32[]{:S(2)}) %all-to-all-start.3) | async-done | bytes 393248 | tf_op jit(solution)/shard_map/all_to_all | solution.py:180
  187.3 24.6 %collective-permute-start.1 = (bf16[128,4096]{1,0:T(8,128)(2,1)}, bf16[128,4096]{1,0:T(8,128)(2,1)S(1)}, u32[]{:S(2)}, u32[]{:S(2)}) collective-permute-start(bf16[128,4096]{1,0:T(8,128)(2,1)} %get-tuple-element.418), channel_id=1, source_target_pairs={{0,32},{32,64},{64,96},{1,33},{33,65},{65,97},{2,34},{34,66},{66,9... | collective-permute-start | bytes 3145736 | tf_op jit(solution)/shard_map/ppermute | solution.py:12
  211.9 22.9 %collective-permute-done.1 = bf16[128,4096]{1,0:T(8,128)(2,1)S(1)} collective-permute-done((bf16[128,4096]{1,0:T(8,128)(2,1)}, bf16[128,4096]{1,0:T(8,128)(2,1)S(1)}, u32[]{:S(2)}, u32[]{:S(2)}) %collective-permute-start.1) | collective-permute-done | bytes 1048608 | tf_op jit(solution)/shard_map/ppermute | solution.py:12
  235.7 4.9 all-to-all-start.4
  240.6 11.8 %all-to-all-done.4 = bf16[32,12,512]{2,1,0:T(8,128)(2,1)} async-done(((bf16[32,12,512]{2,1,0:T(8,128)(2,1)}), bf16[32,12,512]{2,1,0:T(8,128)(2,1)}, u32[]{:S(2)}, u32[]{:S(2)}) %all-to-all-start.4) | async-done | bytes 393248 | tf_op jit(solution)/shard_map/all_to_all | solution.py:175
  259.6 11.4 %all-to-all-done.5 = bf16[32,12,512]{2,1,0:T(8,128)(2,1)} async-done(((bf16[32,12,512]{2,1,0:T(8,128)(2,1)}), bf16[32,12,512]{2,1,0:T(8,128)(2,1)}, u32[]{:S(2)}, u32[]{:S(2)}) %all-to-all-start.5) | async-done | bytes 393248 | tf_op jit(solution)/shard_map/all_to_all | solution.py:180
  272.3 5.0 collective-permute-start.2
  277.3 22.0 %collective-permute-done.2 = bf16[128,4096]{1,0:T(8,128)(2,1)} collective-permute-done((bf16[128,4096]{1,0:T(8,128)(2,1)}, bf16[128,4096]{1,0:T(8,128)(2,1)}, u32[]{:S(2)}, u32[]{:S(2)}) %collective-permute-start.2) | collective-permute-done | bytes 1048608 | tf_op jit(solution)/shard_map/ppermute | solution.py:12
  305.9 10.8 %all-to-all-done.6 = bf16[32,12,512]{2,1,0:T(8,128)(2,1)} async-done(((bf16[32,12,512]{2,1,0:T(8,128)(2,1)}), bf16[32,12,512]{2,1,0:T(8,128)(2,1)}, u32[]{:S(2)}, u32[]{:S(2)}) %all-to-all-start.6) | async-done | bytes 393248 | tf_op jit(solution)/shard_map/all_to_all | solution.py:175
  323.6 8.4 %all-to-all-done.8 = bf16[32,12,512]{2,1,0:T(8,128)(2,1)S(1)} async-done(((bf16[32,12,512]{2,1,0:T(8,128)(2,1)}), bf16[32,12,512]{2,1,0:T(8,128)(2,1)S(1)}, u32[]{:S(2)}, u32[]{:S(2)}) %all-to-all-start.8) | async-done | bytes 393248 | tf_op jit(solution)/shard_map/all_to_all | solution.py:202
  339.0 9.9 %all-to-all-done.9 = bf16[32,12,512]{2,1,0:T(8,128)(2,1)} async-done(((bf16[32,12,512]{2,1,0:T(8,128)(2,1)}), bf16[32,12,512]{2,1,0:T(8,128)(2,1)}, u32[]{:S(2)}, u32[]{:S(2)}) %all-to-all-start.9) | async-done | bytes 393248 | tf_op jit(solution)/shard_map/all_to_all | solution.py:208
  352.0 45.1 %collective-permute-done.3 = bf16[128,4096]{1,0:T(8,128)(2,1)} collective-permute-done((bf16[128,4096]{1,0:T(8,128)(2,1)}, bf16[128,4096]{1,0:T(8,128)(2,1)}, u32[]{:S(2)}, u32[]{:S(2)}) %collective-permute-start.3) | collective-permute-done | bytes 1048608 | tf_op jit(solution)/shard_map/ppermute | solution.py:12
  402.6 11.8 %all-to-all-done.10 = bf16[32,12,512]{2,1,0:T(8,128)(2,1)} async-done(((bf16[32,12,512]{2,1,0:T(8,128)(2,1)}), bf16[32,12,512]{2,1,0:T(8,128)(2,1)}, u32[]{:S(2)}, u32[]{:S(2)}) %all-to-all-start.10) | async-done | bytes 393248 | tf_op jit(solution)/shard_map/all_to_all | solution.py:202
  419.7 11.4 %all-to-all-done.11 = bf16[32,12,512]{2,1,0:T(8,128)(2,1)} async-done(((bf16[32,12,512]{2,1,0:T(8,128)(2,1)}), bf16[32,12,512]{2,1,0:T(8,128)(2,1)}, u32[]{:S(2)}, u32[]{:S(2)}) %all-to-all-start.11) | async-done | bytes 393248 | tf_op jit(solution)/shard_map/all_to_all | solution.py:208
  433.9 26.8 %collective-permute-done.4 = bf16[128,4096]{1,0:T(8,128)(2,1)} collective-permute-done((bf16[128,4096]{1,0:T(8,128)(2,1)}, bf16[128,4096]{1,0:T(8,128)(2,1)}, u32[]{:S(2)}, u32[]{:S(2)}) %collective-permute-start.4) | collective-permute-done | bytes 1048608 | tf_op jit(solution)/shard_map/ppermute | solution.py:12
  466.2 11.8 %all-to-all-done.12 = bf16[32,12,512]{2,1,0:T(8,128)(2,1)} async-done(((bf16[32,12,512]{2,1,0:T(8,128)(2,1)}), bf16[32,12,512]{2,1,0:T(8,128)(2,1)}, u32[]{:S(2)}, u32[]{:S(2)}) %all-to-all-start.12) | async-done | bytes 393248 | tf_op jit(solution)/shard_map/all_to_all | solution.py:202
  483.3 11.4 %all-to-all-done.13 = bf16[32,12,512]{2,1,0:T(8,128)(2,1)} async-done(((bf16[32,12,512]{2,1,0:T(8,128)(2,1)}), bf16[32,12,512]{2,1,0:T(8,128)(2,1)}, u32[]{:S(2)}, u32[]{:S(2)}) %all-to-all-start.13) | async-done | bytes 393248 | tf_op jit(solution)/shard_map/all_to_all | solution.py:208
  504.3 114.2 %collective-permute-done.5 = bf16[128,4096]{1,0:T(8,128)(2,1)} collective-permute-done((bf16[128,4096]{1,0:T(8,128)(2,1)}, bf16[128,4096]{1,0:T(8,128)(2,1)}, u32[]{:S(2)}, u32[]{:S(2)}) %collective-permute-start.5) | collective-permute-done | bytes 1048608 | tf_op jit(solution)/shard_map/ppermute | solution.py:12
  618.5 12.1 %conditional.45 = (bf16[32,12,512]{2,1,0:T(8,128)(2,1)}) conditional(s32[]{:T(128)} %convert_element_type.258, () %tuple.197, (s32[256]{0:T(256)S(1)}, f32[128,2]{1,0:T(8,128)S(1)}, bf16[128,4096]{1,0:T(8,128)(2,1)}, bf16[512,4096]{1,0:T(8,128)(2,1)}) %tuple.293), branch_computations={%region_69.71_spmd, %region_70.73_spmd} | conditional | flops 537264896 | bytes 9049098 | solution.py:199
  636.3 10.6 %all-to-all-done.14 = bf16[32,12,512]{2,1,0:T(8,128)(2,1)} async-done(((bf16[32,12,512]{2,1,0:T(8,128)(2,1)}), bf16[32,12,512]{2,1,0:T(8,128)(2,1)}, u32[]{:S(2)}, u32[]{:S(2)}) %all-to-all-start.14) | async-done | bytes 393248 | tf_op jit(solution)/shard_map/all_to_all | solution.py:202
  647.0 9.2 %conditional.46 = (bf16[384,512]{1,0:T(8,128)(2,1)S(1)}) conditional(s32[]{:T(128)} %convert_element_type.258, () %tuple.196, (bf16[32,12,512]{2,1,0:T(8,128)(2,1)}, bf16[1024,512]{1,0:T(8,128)(2,1)}, bf16[384,512]{1,0:T(8,128)(2,1)}, bf16[512,2048]{1,0:T(8,128)(2,1)S(1)}) %tuple.305), branch_computations={%region_72.74_spmd, %region_73.75_spmd} | conditional | flops 2021720064 | bytes 16646152 | solution.py:207
  663.2 9.1 %all-to-all-done.15 = bf16[32,12,512]{2,1,0:T(8,128)(2,1)S(1)} async-done(((bf16[32,12,512]{2,1,0:T(8,128)(2,1)}), bf16[32,12,512]{2,1,0:T(8,128)(2,1)S(1)}, u32[]{:S(2)}, u32[]{:S(2)}) %all-to-all-start.15) | async-done | bytes 393248 | tf_op jit(solution)/shard_map/all_to_all | solution.py:208
  672.3 9.3 %conditional.47 = (bf16[128,4096]{1,0:T(8,128)(2,1)}) conditional(s32[]{:T(128)} %convert_element_type.258, () %tuple.177, (bf16[128,4096]{1,0:T(8,128)(2,1)}, bf16[128,4096]{1,0:T(8,128)(2,1)S(1)}, f32[128,2]{1,0:T(8,128)S(1)}, bf16[32,12,512]{2,1,0:T(8,128)(2,1)S(1)}, s32[256]{0:T(256)S(1)}, /*index=5*/bf16[4096,512]{1,0:T(8,128)(2,1)}) %tuple.297), branch_computations={%region_74.76_spmd, %region_75.80_spmd} | conditional | flops 545197440 | bytes 17579016 | solution.py:215
  (165 shorter events, 172.0 us)
Async XLA Ops:
  7.2 52.7 %all-gather.3.cloned.1.call-start = ((), (), s32[]{:S(2)}) async-start(), calls=%async_computation.16 | async-start | bytes 4325376 | tf_op jit(solution)/shard_map/all_gather | solution.py:70
  7.9 104.5 %all-gather.5.cloned.1.call-start = ((), (), s32[]{:S(2)}) async-start(), calls=%async_computation.17 | async-start | bytes 4325376 | tf_op jit(solution)/shard_map/all_gather | solution.py:71
  59.9 26.6 %copy-start = (bf16[1,1,512,2048]{3,2,1,0:T(8,128)(2,1)S(1)}, bf16[1,1,512,2048]{3,2,1,0:T(8,128)(2,1)}, u32[]{:S(2)}) copy-start(bf16[1,1,512,2048]{3,2,1,0:T(8,128)(2,1)} %param.63) | copy-start | bytes 6291460
  67.6 18.0 %all-to-all-start = ((bf16[32,12,512]{2,1,0:T(8,128)(2,1)}), bf16[32,12,512]{2,1,0:T(8,128)(2,1)S(1)}, u32[]{:S(2)}, u32[]{:S(2)}) async-start(bf16[32,12,512]{2,1,0:T(8,128)(2,1)} %get-tuple-element.413), calls=%async_computation | async-start | bytes 1048576 | tf_op jit(solution)/shard_map/all_to_all | solution.py:175
  86.5 8.0 %copy-start.15 = (f32[1,128,2]{1,2,0:T(2,128)S(1)}, f32[1,128,2]{1,2,0:T(2,128)}, u32[]{:S(2)}) copy-start(f32[1,128,2]{1,2,0:T(2,128)} %param.66) | copy-start | bytes 3076
  89.2 23.2 %copy-start.1 = (bf16[128,4096]{1,0:T(8,128)(2,1)S(1)}, bf16[128,4096]{1,0:T(8,128)(2,1)}, u32[]{:S(2)}) copy-start(bf16[128,4096]{1,0:T(8,128)(2,1)} %param.59) | copy-start | bytes 3145732
  90.1 22.3 %all-to-all-start.1 = ((bf16[32,12,512]{2,1,0:T(8,128)(2,1)}), bf16[32,12,512]{2,1,0:T(8,128)(2,1)}, u32[]{:S(2)}, u32[]{:S(2)}) async-start(bf16[32,12,512]{2,1,0:T(8,128)(2,1)} %reshape.321), calls=%async_computation.1 | async-start | bytes 1048576 | tf_op jit(solution)/shard_map/all_to_all | solution.py:180
  125.1 24.2 %collective-permute-start = (bf16[128,4096]{1,0:T(8,128)(2,1)}, bf16[128,4096]{1,0:T(8,128)(2,1)S(1)}, u32[]{:S(2)}, u32[]{:S(2)}) collective-permute-start(bf16[128,4096]{1,0:T(8,128)(2,1)} %get-tuple-element.415), channel_id=1, source_target_pairs={{0,32},{32,64},{64,96},{1,33},{33,65},{65,97},{2,34},{34,66},{66,9... | collective-permute-start | bytes 3145736 | tf_op jit(solution)/shard_map/ppermute | solution.py:12
  149.3 36.9 %copy-start.2 = (bf16[128,4096]{1,0:T(8,128)(2,1)}, bf16[128,4096]{1,0:T(8,128)(2,1)S(1)}, u32[]{:S(2)}) copy-start(bf16[128,4096]{1,0:T(8,128)(2,1)S(1)} %collective-permute-done) | copy-start | bytes 3145732
  150.2 16.9 %all-to-all-start.2 = ((bf16[32,12,512]{2,1,0:T(8,128)(2,1)}), bf16[32,12,512]{2,1,0:T(8,128)(2,1)}, u32[]{:S(2)}, u32[]{:S(2)}) async-start(bf16[32,12,512]{2,1,0:T(8,128)(2,1)} %get-tuple-element.416), calls=%async_computation.2 | async-start | bytes 1048576 | tf_op jit(solution)/shard_map/all_to_all | solution.py:175
  170.4 15.8 %all-to-all-start.3 = ((bf16[32,12,512]{2,1,0:T(8,128)(2,1)}), bf16[32,12,512]{2,1,0:T(8,128)(2,1)}, u32[]{:S(2)}, u32[]{:S(2)}) async-start(bf16[32,12,512]{2,1,0:T(8,128)(2,1)} %reshape.323), calls=%async_computation.3 | async-start | bytes 1048576 | tf_op jit(solution)/shard_map/all_to_all | solution.py:180
  187.3 47.5 %collective-permute-start.1 = (bf16[128,4096]{1,0:T(8,128)(2,1)}, bf16[128,4096]{1,0:T(8,128)(2,1)S(1)}, u32[]{:S(2)}, u32[]{:S(2)}) collective-permute-start(bf16[128,4096]{1,0:T(8,128)(2,1)} %get-tuple-element.418), channel_id=1, source_target_pairs={{0,32},{32,64},{64,96},{1,33},{33,65},{65,97},{2,34},{34,66},{66,9... | collective-permute-start | bytes 3145736 | tf_op jit(solution)/shard_map/ppermute | solution.py:12
  234.8 36.2 %copy-start.3 = (bf16[128,4096]{1,0:T(8,128)(2,1)}, bf16[128,4096]{1,0:T(8,128)(2,1)S(1)}, u32[]{:S(2)}) copy-start(bf16[128,4096]{1,0:T(8,128)(2,1)S(1)} %collective-permute-done.1) | copy-start | bytes 3145732
  235.7 16.6 %all-to-all-start.4 = ((bf16[32,12,512]{2,1,0:T(8,128)(2,1)}), bf16[32,12,512]{2,1,0:T(8,128)(2,1)}, u32[]{:S(2)}, u32[]{:S(2)}) async-start(bf16[32,12,512]{2,1,0:T(8,128)(2,1)} %get-tuple-element.419), calls=%async_computation.4 | async-start | bytes 1048576 | tf_op jit(solution)/shard_map/all_to_all | solution.py:175
  255.2 15.8 %all-to-all-start.5 = ((bf16[32,12,512]{2,1,0:T(8,128)(2,1)}), bf16[32,12,512]{2,1,0:T(8,128)(2,1)}, u32[]{:S(2)}, u32[]{:S(2)}) async-start(bf16[32,12,512]{2,1,0:T(8,128)(2,1)} %reshape.325), calls=%async_computation.5 | async-start | bytes 1048576 | tf_op jit(solution)/shard_map/all_to_all | solution.py:180
  272.3 27.0 %collective-permute-start.2 = (bf16[128,4096]{1,0:T(8,128)(2,1)}, bf16[128,4096]{1,0:T(8,128)(2,1)}, u32[]{:S(2)}, u32[]{:S(2)}) collective-permute-start(bf16[128,4096]{1,0:T(8,128)(2,1)} %get-tuple-element.421), channel_id=1, source_target_pairs={{0,32},{32,64},{64,96},{1,33},{33,65},{65,97},{2,34},{34,66},{66,9... | collective-permute-start | bytes 3145736 | tf_op jit(solution)/shard_map/ppermute | solution.py:12
  300.1 16.6 %all-to-all-start.6 = ((bf16[32,12,512]{2,1,0:T(8,128)(2,1)}), bf16[32,12,512]{2,1,0:T(8,128)(2,1)}, u32[]{:S(2)}, u32[]{:S(2)}) async-start(bf16[32,12,512]{2,1,0:T(8,128)(2,1)} %get-tuple-element.422), calls=%async_computation.6 | async-start | bytes 1048576 | tf_op jit(solution)/shard_map/all_to_all | solution.py:175
  316.8 15.2 %all-to-all-start.8 = ((bf16[32,12,512]{2,1,0:T(8,128)(2,1)}), bf16[32,12,512]{2,1,0:T(8,128)(2,1)S(1)}, u32[]{:S(2)}, u32[]{:S(2)}) async-start(bf16[32,12,512]{2,1,0:T(8,128)(2,1)} %copy-done.13), calls=%async_computation.8 | async-start | bytes 1048576 | tf_op jit(solution)/shard_map/all_to_all | solution.py:202
  321.6 10.4 %copy-start.12 = (bf16[384,512]{1,0:T(8,128)(2,1)}, bf16[384,512]{1,0:T(8,128)(2,1)S(1)}, u32[]{:S(2)}) copy-start(bf16[384,512]{1,0:T(8,128)(2,1)S(1)} %reshape.326) | copy-start | bytes 1179652
  332.9 16.0 %all-to-all-start.9 = ((bf16[32,12,512]{2,1,0:T(8,128)(2,1)}), bf16[32,12,512]{2,1,0:T(8,128)(2,1)}, u32[]{:S(2)}, u32[]{:S(2)}) async-start(bf16[32,12,512]{2,1,0:T(8,128)(2,1)} %reshape.328), calls=%async_computation.9 | async-start | bytes 1048576 | tf_op jit(solution)/shard_map/all_to_all | solution.py:208
  350.7 46.4 %collective-permute-start.3 = (bf16[128,4096]{1,0:T(8,128)(2,1)}, bf16[128,4096]{1,0:T(8,128)(2,1)}, u32[]{:S(2)}, u32[]{:S(2)}) collective-permute-start(bf16[128,4096]{1,0:T(8,128)(2,1)} %get-tuple-element.427), channel_id=1, source_target_pairs={{32,0},{64,32},{96,64},{33,1},{65,33},{97,65},{34,2},{66,34},{98,6... | collective-permute-start | bytes 3145736 | tf_op jit(solution)/shard_map/ppermute | solution.py:12
  398.0 16.4 %all-to-all-start.10 = ((bf16[32,12,512]{2,1,0:T(8,128)(2,1)}), bf16[32,12,512]{2,1,0:T(8,128)(2,1)}, u32[]{:S(2)}, u32[]{:S(2)}) async-start(bf16[32,12,512]{2,1,0:T(8,128)(2,1)} %get-tuple-element.428), calls=%async_computation.10 | async-start | bytes 1048576 | tf_op jit(solution)/shard_map/all_to_all | solution.py:202
  415.3 15.8 %all-to-all-start.11 = ((bf16[32,12,512]{2,1,0:T(8,128)(2,1)}), bf16[32,12,512]{2,1,0:T(8,128)(2,1)}, u32[]{:S(2)}, u32[]{:S(2)}) async-start(bf16[32,12,512]{2,1,0:T(8,128)(2,1)} %reshape.329), calls=%async_computation.11 | async-start | bytes 1048576 | tf_op jit(solution)/shard_map/all_to_all | solution.py:208
  432.6 28.1 %collective-permute-start.4 = (bf16[128,4096]{1,0:T(8,128)(2,1)}, bf16[128,4096]{1,0:T(8,128)(2,1)}, u32[]{:S(2)}, u32[]{:S(2)}) collective-permute-start(bf16[128,4096]{1,0:T(8,128)(2,1)} %get-tuple-element.430), channel_id=1, source_target_pairs={{32,0},{64,32},{96,64},{33,1},{65,33},{97,65},{34,2},{66,34},{98,6... | collective-permute-start | bytes 3145736 | tf_op jit(solution)/shard_map/ppermute | solution.py:12
  461.6 16.4 %all-to-all-start.12 = ((bf16[32,12,512]{2,1,0:T(8,128)(2,1)}), bf16[32,12,512]{2,1,0:T(8,128)(2,1)}, u32[]{:S(2)}, u32[]{:S(2)}) async-start(bf16[32,12,512]{2,1,0:T(8,128)(2,1)} %get-tuple-element.431), calls=%async_computation.12 | async-start | bytes 1048576 | tf_op jit(solution)/shard_map/all_to_all | solution.py:202
  478.9 15.8 %all-to-all-start.13 = ((bf16[32,12,512]{2,1,0:T(8,128)(2,1)}), bf16[32,12,512]{2,1,0:T(8,128)(2,1)}, u32[]{:S(2)}, u32[]{:S(2)}) async-start(bf16[32,12,512]{2,1,0:T(8,128)(2,1)} %reshape.330), calls=%async_computation.13 | async-start | bytes 1048576 | tf_op jit(solution)/shard_map/all_to_all | solution.py:208
  495.9 122.6 %collective-permute-start.5 = (bf16[128,4096]{1,0:T(8,128)(2,1)}, bf16[128,4096]{1,0:T(8,128)(2,1)}, u32[]{:S(2)}, u32[]{:S(2)}) collective-permute-start(bf16[128,4096]{1,0:T(8,128)(2,1)} %get-tuple-element.433), channel_id=1, source_target_pairs={{32,0},{64,32},{96,64},{33,1},{65,33},{97,65},{34,2},{66,34},{98,6... | collective-permute-start | bytes 3145736 | tf_op jit(solution)/shard_map/ppermute | solution.py:12
  497.2 121.3 %copy-start.5 = (f32[128,2]{1,0:T(8,128)S(1)}, f32[128,2]{1,0:T(8,128)}, u32[]{:S(2)}) copy-start(f32[128,2]{1,0:T(8,128)} %bitcast_multiply_fusion) | copy-start | bytes 3076
  499.9 130.7 %all-to-all-start.7 = ((bf16[32,12,512]{2,1,0:T(8,128)(2,1)}), bf16[32,12,512]{2,1,0:T(8,128)(2,1)}, u32[]{:S(2)}, u32[]{:S(2)}) async-start(bf16[32,12,512]{2,1,0:T(8,128)(2,1)} %reshape.327), calls=%async_computation.7 | async-start | bytes 1048576 | tf_op jit(solution)/shard_map/all_to_all | solution.py:180
  630.6 16.4 %all-to-all-start.14 = ((bf16[32,12,512]{2,1,0:T(8,128)(2,1)}), bf16[32,12,512]{2,1,0:T(8,128)(2,1)}, u32[]{:S(2)}, u32[]{:S(2)}) async-start(bf16[32,12,512]{2,1,0:T(8,128)(2,1)} %get-tuple-element.434), calls=%async_computation.14 | async-start | bytes 1048576 | tf_op jit(solution)/shard_map/all_to_all | solution.py:202
  657.1 15.2 %all-to-all-start.15 = ((bf16[32,12,512]{2,1,0:T(8,128)(2,1)}), bf16[32,12,512]{2,1,0:T(8,128)(2,1)S(1)}, u32[]{:S(2)}, u32[]{:S(2)}) async-start(bf16[32,12,512]{2,1,0:T(8,128)(2,1)} %reshape.331), calls=%async_computation.15 | async-start | bytes 1048576 | tf_op jit(solution)/shard_map/all_to_all | solution.py:208
  660.8 11.5 %copy-start.14 = (f32[128,2]{1,0:T(8,128)S(1)}, f32[128,2]{1,0:T(8,128)}, u32[]{:S(2)}) copy-start(f32[128,2]{1,0:T(8,128)} %broadcast_in_dim.120) | copy-start | bytes 3076
  (5 other events, 18.9 us)
Sparse Core Ops, SparseCore 0:
  10.3 49.5 all-gather.2
  62.1 50.2 all-gather.4
where the time goes:
time: 702 us; the launch traced here: 691 us
  waiting for transfers between devices  475 us (68%)
  starting transfers between devices  107 us (15%)
  local copies, waits for them, and re-layouts  45 us (6%)
  matrix products  25.5 us (4%)
  other arithmetic  21.7 us (3%)
  between operations  15.4 us (2%)
    ppermute x6, waiting for transfers between devices, shifted(): return lax.ppermute(block, axis, route)  254 us
    all_to_all x8, waiting for transfers between devices, body(): lax.all_to_all(send, 'expert', split_axis=0, concat_axis=0, tiled=True)  89.7 us
    all_gather x1, waiting for transfers between devices, body(): lax.all_gather(w_down, 'expert', axis=1, tiled=True)  48 us
    all_to_all x4, waiting for transfers between devices, body(): lax.all_to_all(lat_rows.reshape(experts, capacity, latent_width), 'expert...  41.8 us
    all_to_all x8, starting transfers between devices, body(): lax.all_to_all(send, 'expert', split_axis=0, concat_axis=0, tiled=True)  37.7 us
    ppermute x6, starting transfers between devices, shifted(): return lax.ppermute(block, axis, route)  34.8 us
    all_to_all x4, waiting for transfers between devices, body(): lax.all_to_all(outcome.reshape(experts, capacity, latent_width), 'expert'...  22.8 us
    all_to_all x4, starting transfers between devices, body(): lax.all_to_all(outcome.reshape(experts, capacity, latent_width), 'expert'...  17.6 us
  transfers between devices with their start and end apart: 24, of which 22 were waited for; matrix products, arithmetic and copies ran while one was open for 6% of the time, Pallas kernels for 0%

commit v1 on v0

v1 whole, which is shorter than its diff:
```python
import functools

import jax
import jax.numpy as jnp
from jax import lax
from jax.experimental import pallas as pl
from jax.experimental.pallas import tpu as pltpu
from jax.sharding import PartitionSpec as P

EPS = 1e-05
MESH = pl.DeviceIdType.MESH
BF = jnp.bfloat16
F32 = jnp.float32
SLOT = 16


def dot(a, b):
    return jnp.dot(a, b, preferred_element_type=F32)


def dot_t(a, b):
    return lax.dot_general(a, b, (((1,), (1,)), ((), ())), preferred_element_type=F32)


def kernel(
    sections, experts,
    tokens, cot, w_down, w_up, w_gu, w_o, routes, gates, counts,
    out, gin,
    up_full, down_full, down_first,
    x_in, g_in, g_new, g_fin,
    gate_f, up_f, hidden, joined,
    send_a, recv_a, send_b, recv_b, send_c, recv_c, send_d, recv_d,
    put, take0, take1,
    lat_in, lat_out, lg_in, lg_out, lat_f, inv_f,
    zs, zr, us, ur, ds, dr, fs, fr, as_, ar, hs, hr, loc,
):
    t = lax.axis_index("section")
    e = lax.axis_index("expert")
    x = e // 8
    y = (e // 2) % 4
    c = e % 2
    above = (t + 1) % sections
    below = (t + sections - 1) % sections
    toks, width = tokens.shape
    lat_w = lat_in.shape[1]
    ffh = w_o.shape[2]
    last = sections - 1

    def at(xx, yy, cc):
        return (t, (xx * 4 + yy) * 2 + cc)

    def send(src, dst, ssem, rsem, dev):
        pltpu.make_async_remote_copy(
            src_ref=src, dst_ref=dst, send_sem=ssem, recv_sem=rsem, device_id=dev, device_id_type=MESH
        ).start()

    def wait(ref, sem):
        pltpu.make_async_copy(ref, ref, sem).wait()

    barrier = pltpu.get_barrier_semaphore()

    def greet(k, carry):
        pl.semaphore_signal(barrier, inc=1, device_id=(t, (e + k) % experts), device_id_type=MESH)
        return carry

    lax.fori_loop(1, experts, greet, 0)
    pl.semaphore_signal(barrier, inc=1, device_id=(above, e), device_id_type=MESH)
    pl.semaphore_signal(barrier, inc=1, device_id=(below, e), device_id_type=MESH)
    pl.semaphore_wait(barrier, experts + 1)

    def first(buf, ha, hb, ss, rs):
        for d in range(1, 4):
            blk = buf.at[(x, y, c) + ha]
            send(blk, blk, ss.at[0], rs.at[0], at((x + d) % 4, y, c))
            blk = buf.at[(x, y, c) + hb]
            send(blk, blk, ss.at[1], rs.at[1], at(x, (y + d) % 4, c))

    def second(buf, ha, hb, ss, rs):
        wait(buf.at[(pl.ds(0, 3), 0, 0) + ha], rs.at[0])
        wait(buf.at[(pl.ds(0, 3), 0, 0) + hb], rs.at[1])
        for d in range(1, 4):
            blk = buf.at[(slice(None), y, c) + ha]
            send(blk, blk, ss.at[2], rs.at[2], at(x, (y + d) % 4, c))
            blk = buf.at[(x, slice(None), c) + hb]
            send(blk, blk, ss.at[3], rs.at[3], at((x + d) % 4, y, c))

    def third(buf, ha, hb, ss, rs):
        wait(buf.at[(pl.ds(0, 3), slice(None), 0) + ha], rs.at[2])
        wait(buf.at[(pl.ds(0, 3), slice(None), 0) + hb], rs.at[3])
        blk = buf.at[:, :, c]
        send(blk, blk, ss.at[4], rs.at[4], at(x, y, 1 - c))

    def fourth(buf, ss, rs):
        wait(buf.at[:, :, 0], rs.at[4])

    def gather_done(buf, ha, hb, ss):
        wait(buf.at[(pl.ds(0, 3), 0, 0) + ha], ss.at[0])
        wait(buf.at[(pl.ds(0, 3), 0, 0) + hb], ss.at[1])
        wait(buf.at[(pl.ds(0, 3), slice(None), 0) + ha], ss.at[2])
        wait(buf.at[(pl.ds(0, 3), slice(None), 0) + hb], ss.at[3])
        wait(buf.at[:, :, 0], ss.at[4])

    half_cols = width // 2
    u_a = (slice(None), pl.ds(0, half_cols))
    u_b = (slice(None), pl.ds(half_cols, half_cols))
    half_rows = w_down.shape[1] // 2
    d_a = (pl.ds(0, half_rows), slice(None))
    d_b = (pl.ds(half_rows, half_rows), slice(None))

    send(w_down.at[0], down_full.at[x, y, c], zs.at[0], zr.at[0], (below, e))
    up_full[x, y, c] = w_up[0]
    first(up_full, u_a, u_b, us, ur)
    wait(w_down.at[0], zr.at[0])
    first(down_full, d_a, d_b, ds, dr)

    @pl.when(t == 0)
    def _():
        x_in[...] = tokens[...]

    @pl.when(t == last - 1)
    def _():
        g_in[...] = cot[...]

    count = counts[...]
    expert_lane = lax.broadcasted_iota(jnp.int32, (toks, experts), 1)
    live = lax.broadcasted_iota(jnp.int32, (toks, experts), 0) < count
    one0 = jnp.where((routes[0, :, 0:1] == expert_lane) & live, 1.0, 0.0).astype(F32)
    one1 = jnp.where((routes[0, :, 1:2] == expert_lane) & live, 1.0, 0.0).astype(F32)
    below_diag = jnp.where(
        lax.broadcasted_iota(jnp.int32, (toks, toks), 0) > lax.broadcasted_iota(jnp.int32, (toks, toks), 1), 1.0, 0.0
    ).astype(BF)
    before = dot(below_diag, (one0 + one1).astype(BF))
    slots = experts * SLOT
    spread = jnp.where(
        lax.broadcasted_iota(jnp.int32, (experts, slots), 1) // SLOT
        == lax.broadcasted_iota(jnp.int32, (experts, slots), 0),
        1.0,
        0.0,
    ).astype(BF)
    slot_no = (lax.broadcasted_iota(jnp.int32, (toks, slots), 1) % SLOT).astype(F32)
    here = dot(before.astype(BF), spread) == slot_no
    pick0 = jnp.where(here, dot(one0.astype(BF), spread), 0.0)
    pick1 = jnp.where(here, dot(one1.astype(BF), spread), 0.0)
    take0[...] = pick0.astype(BF)
    take1[...] = pick1.astype(BF)
    put[:, 0:toks] = pick0.T.astype(BF)
    put[:, toks : 2 * toks] = pick1.T.astype(BF)
    gate0 = gates[0, :, 0:1]
    gate1 = gates[0, :, 1:2]

    second(down_full, d_a, d_b, ds, dr)
    second(up_full, u_a, u_b, us, ur)
    third(down_full, d_a, d_b, ds, dr)
    fourth(down_full, ds, dr)

    chunk = 512
    n_chunks = width // chunk

    def up_chunk(j):
        return up_full[:, :, :, :, j * chunk : (j + 1) * chunk].reshape(lat_w, chunk)

    def down_chunk(buf, j):
        return buf[j // 2, 2 * (j % 2) : 2 * (j % 2) + 2].reshape(chunk, lat_w)

    @pl.when(t == last)
    def _():
        total = jnp.zeros((toks, lat_w), F32)
        square = jnp.zeros((toks, 1), F32)
        for j in range(n_chunks):
            part = tokens[:, j * chunk : (j + 1) * chunk]
            total += dot(part, down_chunk(down_full, j))
            wide = part.astype(F32)
            square += jnp.sum(wide * wide, axis=1, keepdims=True)
        inv = lax.rsqrt(square / width + EPS)
        lat_out[...] = (total * inv).astype(BF)
        send(lat_out, lat_in, hs.at[0], hr.at[0], (above, e))

    third(up_full, u_a, u_b, us, ur)
    fourth(up_full, us, ur)

    def exchange(src, dst, k):
        mine = pl.ds(pl.multiple_of(e * SLOT, SLOT), SLOT)
        dst[mine] = src[mine]

        def go(i, carry):
            p = (e + i) % experts
            theirs = pl.ds(pl.multiple_of(p * SLOT, SLOT), SLOT)
            send(src.at[theirs], dst.at[mine], as_.at[k], ar.at[k], (t, p))
            return carry

        lax.fori_loop(1, experts, go, 0)

    def arrived(buf, k):
        wait(buf.at[pl.ds(0, (experts - 1) * SLOT)], ar.at[k])

    def route_grads(mix_grad):
        mg = mix_grad.astype(BF).astype(F32)
        both = jnp.concatenate([(gate0 * mg).astype(BF), (gate1 * mg).astype(BF)], axis=0)
        send_c[...] = dot(put[...], both).astype(BF)
        exchange(send_c, recv_c, 2)

    @pl.when(t == last)
    def _():
        mix_grad = jnp.zeros((toks, lat_w), F32)
        for j in range(n_chunks):
            mix_grad += dot_t(cot[:, j * chunk : (j + 1) * chunk], up_chunk(j))
        route_grads(mix_grad)

    wait(lat_in, hr.at[0])
    lat = lat_in[...]
    send_a[...] = dot(put[...], jnp.concatenate([lat, lat], axis=0)).astype(BF)
    exchange(send_a, recv_a, 0)
    arrived(recv_a, 0)
    rows = recv_a[...]
    part = 256
    for j in range(ffh // part):
        lo = j * part
        a = dot(rows, w_gu[0, 0, :, lo : lo + part])
        u = dot(rows, w_gu[0, 0, :, ffh + lo : ffh + lo + part])
        sig = 1.0 / (1.0 + jnp.exp(-a))
        silu = a * sig
        hidden[:, lo : lo + part] = (silu * u).astype(BF)
        up_f[:, lo : lo + part] = silu
        gate_f[:, lo : lo + part] = u * sig * (1.0 + a * (1.0 - sig))
    send_b[...] = dot(hidden[...], w_o[0, 0]).astype(BF)
    exchange(send_b, recv_b, 1)

    def boundary_grad(lg, dn, x_ref, inv, lat_prod, g_ref, out_ref, mix):
        dotted = jnp.sum(lg.astype(F32) * lat_prod, axis=1, keepdims=True) / width
        scale = inv * inv * dotted
        mix_grad = jnp.zeros((toks, lat_w), F32)
        for j in range(n_chunks):
            cols = slice(j * chunk, (j + 1) * chunk)
            ng = dot_t(lg, down_chunk(dn, j))
            new = (g_ref[:, cols].astype(F32) + inv * ng - scale * x_ref[:, cols].astype(F32)).astype(BF)
            out_ref[:, cols] = new
            if mix:
                mix_grad += dot_t(new, up_chunk(j))
        return mix_grad

    def forward_finish():
        arrived(recv_b, 1)
        back = recv_b[...]
        mixed = (gate0 * dot(take0[...], back) + gate1 * dot(take1[...], back)).astype(BF)

        @pl.when(t > 0)
        def _():
            wait(x_in, hr.at[1])

        total = jnp.zeros((toks, lat_w), F32)
        square = jnp.zeros((toks, 1), F32)
        for j in range(n_chunks):
            cols = slice(j * chunk, (j + 1) * chunk)
            new = (x_in[:, cols].astype(F32) + dot(mixed, up_chunk(j))).astype(BF)
            out[0, :, cols] = new
            wide = new.astype(F32)
            square += jnp.sum(wide * wide, axis=1, keepdims=True)
            total += dot(new, down_chunk(down_full, j))
        inv = lax.rsqrt(square / width + EPS)
        lat_next = total * inv
        lat_f[...] = lat_next
        inv_f[...] = jnp.broadcast_to(inv, inv_f.shape)

        @pl.when(t < last)
        def _():
            lat_out[...] = lat_next.astype(BF)
            send(lat_out, lat_in, hs.at[0], hr.at[0], (above, e))
            send(out.at[0], x_in, hs.at[1], hr.at[1], (above, e))

        @pl.when(t == 0)
        def _():
            down_first[x, y, c] = w_down[0]
            first(down_first, d_a, d_b, fs, fr)
            second(down_first, d_a, d_b, fs, fr)
            third(down_first, d_a, d_b, fs, fr)
            fourth(down_first, fs, fr)
            gather_done(down_first, d_a, d_b, fs)

    def backward():
        @pl.when(t < last)
        def _():
            wait(lg_in, hr.at[2])

            @pl.when(t < last - 1)
            def _():
                wait(g_in, hr.at[3])

            mix_grad = boundary_grad(
                lg_in[...], down_full, out.at[0], inv_f[:, 0:1], lat_f[...], g_in, g_new, True
            )
            route_grads(mix_grad)
            send(g_new, g_fin, hs.at[4], hr.at[4], (above, e))

            @pl.when(t > 0)
            def _():
                send(g_new, g_in, hs.at[3], hr.at[3], (below, e))

        arrived(recv_c, 2)
        grads = recv_c[...]
        for j in range(ffh // part):
            lo = j * part
            hg = dot_t(grads, w_o[0, 0, lo : lo + part, :])
            joined[:, lo : lo + part] = (hg * gate_f[:, lo : lo + part]).astype(BF)
            joined[:, ffh + lo : ffh + lo + part] = (hg * up_f[:, lo : lo + part]).astype(BF)
        send_d[...] = dot_t(joined[...], w_gu[0, 0]).astype(BF)
        exchange(send_d, recv_d, 3)
        arrived(recv_d, 3)
        back = recv_d[...]
        lg_out[...] = (dot(take0[...], back) + dot(take1[...], back)).astype(BF)

        @pl.when(t > 0)
        def _():
            send(lg_out, lg_in, hs.at[2], hr.at[2], (below, e))

    def stage(i, carry):
        @pl.when((i == 0) == (t == last))
        def _():
            backward()

        @pl.when(i == 0)
        def _():
            forward_finish()

        return carry

    lax.fori_loop(0, 2, stage, 0)

    @pl.when(t == 0)
    def _():
        square = jnp.zeros((toks, 1), F32)
        for j in range(n_chunks):
            wide = tokens[:, j * chunk : (j + 1) * chunk].astype(F32)
            square += jnp.sum(wide * wide, axis=1, keepdims=True)
        inv = lax.rsqrt(square / width + EPS)
        boundary_grad(
            lg_out[...], down_first, tokens, inv, lat_in[...].astype(F32), g_new, gin.at[0], False
        )

    @pl.when(t > 0)
    def _():
        wait(g_fin, hr.at[4])
        gin[0] = g_fin[...]

    wait(w_down.at[0], zs.at[0])
    gather_done(up_full, u_a, u_b, us)
    gather_done(down_full, d_a, d_b, ds)
    for k in range(4):
        wait(recv_a.at[pl.ds(0, (experts - 1) * SLOT)], as_.at[k])
    wait(lat_out, hs.at[0])

    @pl.when(t < last)
    def _():
        wait(x_in, hs.at[1])
        wait(g_new, hs.at[4])

    @pl.when(t > 0)
    def _():
        wait(lg_out, hs.at[2])

        @pl.when(t < last)
        def _():
            wait(g_new, hs.at[3])


def body(sections, experts, tokens, cot, w_down, w_up, w_gu, w_o, routes, gates, counts):
    toks, width = tokens.shape
    lat_w = w_down.shape[2]
    ffh = w_o.shape[2]
    slots = experts * SLOT
    vm = pltpu.VMEM
    dma = pltpu.SemaphoreType.DMA
    rows = [vm((slots, lat_w), BF) for _ in range(8)]
    spec = pl.BlockSpec(memory_space=pltpu.VMEM)
    shape = jax.ShapeDtypeStruct((1, toks, width), BF)
    return pl.pallas_call(
        functools.partial(kernel, sections, experts),
        out_shape=(shape, shape),
        in_specs=[spec] * 9,
        out_specs=(spec, spec),
        scratch_shapes=[
            vm((4, 4, 2, lat_w // experts, width), BF),
            vm((4, 4, 2, width // experts, lat_w), BF),
            vm((4, 4, 2, width // experts, lat_w), BF),
            vm((toks, width), BF),
            vm((toks, width), BF),
            vm((toks, width), BF),
            vm((toks, width), BF),
            vm((slots, ffh), F32),
            vm((slots, ffh), F32),
            vm((slots, ffh), BF),
            vm((slots, 2 * ffh), BF),
            *rows,
            vm((slots, 2 * toks), BF),
            vm((toks, slots), BF),
            vm((toks, slots), BF),
            vm((toks, lat_w), BF),
            vm((toks, lat_w), BF),
            vm((toks, lat_w), BF),
            vm((toks, lat_w), BF),
            vm((toks, lat_w), F32),
            vm((toks, 128), F32),
            dma((1,)), dma((1,)),
            dma((5,)), dma((5,)),
            dma((5,)), dma((5,)),
            dma((5,)), dma((5,)),
            dma((4,)), dma((4,)),
            dma((5,)), dma((5,)),
            dma((1,)),
        ],
        compiler_params=pltpu.CompilerParams(
            collective_id=0, has_side_effects=True, vmem_limit_bytes=56 * 1024 * 1024
        ),
    )(tokens, cot, w_down, w_up, w_gu, w_o, routes, gates, counts)


def solution(mesh):
    in_specs = (
        P("expert", None),
        P("expert", None),
        P("section", "expert", None),
        P("section", "expert", None),
        P("section", "expert", None, None),
        P("section", "expert", None, None),
        P("section", "expert", None),
        P("section", "expert", None),
        P("section", "expert"),
    )
    out_specs = (P("section", "expert", None), P("section", "expert", None))
    step = functools.partial(body, mesh.shape["section"], mesh.shape["expert"])
    return jax.shard_map(step, mesh=mesh, in_specs=in_specs, out_specs=out_specs, check_vma=False)
```

time: 702 us -> 258 us (0.37); the launches traced: 691 us -> 256 us
  waiting for transfers between devices: 475 us -> 0 us
  Pallas kernels: 0 us -> 249 us
  starting transfers between devices: 107 us -> 0 us
  local copies, waits for them, and re-layouts: 45 us -> 6.18 us
  matrix products: 25.5 us -> 0 us
  other arithmetic: 21.7 us -> 0 us
  between operations: 15.4 us -> 1.29 us
    ppermute x6 -> x0, waiting for transfers between devices: 254 us -> none  [shifted(): return lax.ppermute(block, axis, route)]
    pallas_call x0 -> x1, Pallas kernels: none -> 249 us  [body(): pl.pallas_call(functools.partial(kernel, sections, experts), out_shape=(s...]
    all_to_all x16 -> x0, waiting for transfers between devices: 154 us -> none  [the longest x8 89.7 us: body(): lax.all_to_all(send, 'expert', split_axis=0, concat_axis=0, tiled=True)]
    all_to_all x16 -> x0, starting transfers between devices: 72.4 us -> none  [the longest x8 37.7 us: body(): lax.all_to_all(send, 'expert', split_axis=0, concat_axis=0, tiled=True)]
    all_gather x2 -> x0, waiting for transfers between devices: 65.1 us -> none  [the longest x1 48 us: body(): lax.all_gather(w_down, 'expert', axis=1, tiled=True)]
    ppermute x6 -> x0, starting transfers between devices: 34.8 us -> none  [shifted(): return lax.ppermute(block, axis, route)]
    dot_general x9 -> x0, matrix products: 25.5 us -> none  [the longest x1 4.04 us: backward_prepare(): lax.dot_general(grad, proj_up, (((1,), (1,)), ((), ())), preferred_elemen...]
    reshape x21 -> x0, local copies, waits for them, and re-layouts: 21.6 us -> none  [the longest x4 5.76 us: body(): rows = arrived_rows.reshape(slots, latent_width)]
  transfers between devices with their start and end apart: 24 -> 0, of which waited for: 22 -> 0; matrix products, arithmetic and copies ran while one was open for 6% -> 0% of each run, Pallas kernels for 0% -> 0%
where the time goes in v1:
time: 258 us; the launch traced here: 256 us
  Pallas kernels  249 us (97%)
  local copies, waits for them, and re-layouts  6.18 us (2%)
    pallas_call x1, Pallas kernels, body(): pl.pallas_call(functools.partial(kernel, sections, experts), out_shape=(s...  249 us
    unnamed x6, local copies, waits for them, and re-layouts  6.18 us

profile of v1, /device:TPU:1, one launch (start us, length us, event | category | flops | bytes accessed | tf_op | source)
XLA Modules:
  0.0 256.5 jit_solution(5421602064475479715)
XLA Ops:
  1.3 1.4 copy.11.routes
  2.7 1.4 copy.12.gates
  4.1 249.0 %shard_map.104 = (bf16[1,128,4096]{2,1,0:T(8,128)(2,1)}, bf16[1,128,4096]{2,1,0:T(8,128)(2,1)}) custom-call(bf16[128,4096]{1,0:T(8,128)(2,1)} %tokens.1, bf16[128,4096]{1,0:T(8,128)(2,1)} %cot.1, bf16[1,128,512]{2,1,0:T(8,128)(2,1)} %w_down.1, bf16[1,16,4096]{2,1,0:T(8,128)(2,1)} %w_up.1, bf16[1,1,512,2048]{3,2,1,0:T(8,128)(2,1)} %w_gu.1, ...), custom_call_target="tpu_custom_call" | custom-call | tf_op jit(solution)/shard_map/pallas_call | solution.py:375
  253.1 0.0 copy-start
  253.1 2.4 copy.16
  255.5 0.0 copy-done
  255.5 1.0 copy.17
Async XLA Ops:
  253.1 2.4 copy-start

commit v2 on v1

--- a/solution.py
+++ b/solution.py
@@ -12,6 +12,12 @@
 BF = jnp.bfloat16
 F32 = jnp.float32
 SLOT = 16
+GROUPS = 2
+PER = 32 // GROUPS
+ORDER = sorted(
+    [(dx, dy, dc) for dx in range(4) for dy in range(4) for dc in range(2) if (dx, dy, dc) != (0, 0, 0)],
+    key=lambda k: -(min(k[0], 4 - k[0]) + min(k[1], 4 - k[1])),
+)
 
 
 def dot(a, b):
@@ -124,8 +130,11 @@
     count = counts[...]
     expert_lane = lax.broadcasted_iota(jnp.int32, (toks, experts), 1)
     live = lax.broadcasted_iota(jnp.int32, (toks, experts), 0) < count
-    one0 = jnp.where((routes[0, :, 0:1] == expert_lane) & live, 1.0, 0.0).astype(F32)
-    one1 = jnp.where((routes[0, :, 1:2] == expert_lane) & live, 1.0, 0.0).astype(F32)
+    def column(row):
+        return jnp.broadcast_to(row, (toks, toks)).T
+
+    one0 = jnp.where((column(routes[0, 0:1])[:, 0:experts] == expert_lane) & live, 1.0, 0.0).astype(F32)
+    one1 = jnp.where((column(routes[0, 1:2])[:, 0:experts] == expert_lane) & live, 1.0, 0.0).astype(F32)
     below_diag = jnp.where(
         lax.broadcasted_iota(jnp.int32, (toks, toks), 0) > lax.broadcasted_iota(jnp.int32, (toks, toks), 1), 1.0, 0.0
     ).astype(BF)
@@ -145,8 +154,8 @@
     take1[...] = pick1.astype(BF)
     put[:, 0:toks] = pick0.T.astype(BF)
     put[:, toks : 2 * toks] = pick1.T.astype(BF)
-    gate0 = gates[0, :, 0:1]
-    gate1 = gates[0, :, 1:2]
+    gate0 = column(gates[0, 0:1])[:, 0:1]
+    gate1 = column(gates[0, 1:2])[:, 0:1]
 
     second(down_full, d_a, d_b, ds, dr)
     second(up_full, u_a, u_b, us, ur)
@@ -178,26 +187,35 @@
     third(up_full, u_a, u_b, us, ur)
     fourth(up_full, us, ur)
 
-    def exchange(src, dst, k):
-        mine = pl.ds(pl.multiple_of(e * SLOT, SLOT), SLOT)
-        dst[mine] = src[mine]
-
-        def go(i, carry):
-            p = (e + i) % experts
-            theirs = pl.ds(pl.multiple_of(p * SLOT, SLOT), SLOT)
-            send(src.at[theirs], dst.at[mine], as_.at[k], ar.at[k], (t, p))
-            return carry
-
-        lax.fori_loop(1, experts, go, 0)
+    def block(i):
+        return pl.ds(pl.multiple_of(i * SLOT, SLOT), SLOT)
+
+    def dispatch(src, dst, k):
+        for pos, (dx, dy, dc) in enumerate(ORDER):
+            p = (((x + dx) % 4) * 4 + (y + dy) % 4) * 2 + (c + dc) % 2
+            send(src.at[block(p)], dst.at[block(pos)], as_.at[k], ar.at[k, pos // PER], (t, p))
+        dst[block(experts - 1)] = src[block(e)]
+
+    def give_back(src, dst, k, g):
+        for pos, (dx, dy, dc) in enumerate(ORDER):
+            if pos // PER == g:
+                p = (((x + 4 - dx) % 4) * 4 + (y + 4 - dy) % 4) * 2 + (c + dc) % 2
+                send(src.at[block(pos)], dst.at[block(e)], as_.at[k], ar.at[k, 0], (t, p))
+        if g == GROUPS - 1:
+            dst[block(e)] = src[block(experts - 1)]
+
+    def group_arrived(buf, k, g):
+        size = PER if g < GROUPS - 1 else PER - 1
+        wait(buf.at[pl.ds(0, size * SLOT)], ar.at[k, g])
 
     def arrived(buf, k):
-        wait(buf.at[pl.ds(0, (experts - 1) * SLOT)], ar.at[k])
+        wait(buf.at[pl.ds(0, (experts - 1) * SLOT)], ar.at[k, 0])
 
     def route_grads(mix_grad):
         mg = mix_grad.astype(BF).astype(F32)
         both = jnp.concatenate([(gate0 * mg).astype(BF), (gate1 * mg).astype(BF)], axis=0)
         send_c[...] = dot(put[...], both).astype(BF)
-        exchange(send_c, recv_c, 2)
+        dispatch(send_c, recv_c, 2)
 
     @pl.when(t == last)
     def _():
@@ -209,21 +227,27 @@
     wait(lat_in, hr.at[0])
     lat = lat_in[...]
     send_a[...] = dot(put[...], jnp.concatenate([lat, lat], axis=0)).astype(BF)
-    exchange(send_a, recv_a, 0)
-    arrived(recv_a, 0)
-    rows = recv_a[...]
+    dispatch(send_a, recv_a, 0)
     part = 256
-    for j in range(ffh // part):
-        lo = j * part
-        a = dot(rows, w_gu[0, 0, :, lo : lo + part])
-        u = dot(rows, w_gu[0, 0, :, ffh + lo : ffh + lo + part])
-        sig = 1.0 / (1.0 + jnp.exp(-a))
-        silu = a * sig
-        hidden[:, lo : lo + part] = (silu * u).astype(BF)
-        up_f[:, lo : lo + part] = silu
-        gate_f[:, lo : lo + part] = u * sig * (1.0 + a * (1.0 - sig))
-    send_b[...] = dot(hidden[...], w_o[0, 0]).astype(BF)
-    exchange(send_b, recv_b, 1)
+    height = PER * SLOT
+    for g in range(GROUPS):
+        group_arrived(recv_a, 0, g)
+        span = slice(g * height, (g + 1) * height)
+        rows = recv_a[span]
+        for j in range(ffh // part):
+            lo = j * part
+            a = dot(rows, w_gu[0, 0, :, lo : lo + part])
+            u = dot(rows, w_gu[0, 0, :, ffh + lo : ffh + lo + part])
+            sig = 1.0 / (1.0 + jnp.exp(-a))
+            silu = a * sig
+            hidden[span, lo : lo + part] = (silu * u).astype(BF)
+            up_f[span, lo : lo + part] = silu
+            gate_f[span, lo : lo + part] = u * sig * (1.0 + a * (1.0 - sig))
+        send_b[span] = dot(hidden[span], w_o[0, 0]).astype(BF)
+
+        @pl.when(t < last)
+        def _():
+            give_back(send_b, recv_b, 1, g)
 
     def boundary_grad(lg, dn, x_ref, inv, lat_prod, g_ref, out_ref, mix):
         dotted = jnp.sum(lg.astype(F32) * lat_prod, axis=1, keepdims=True) / width
@@ -239,6 +263,11 @@
         return mix_grad
 
     def forward_finish():
+        @pl.when(t == last)
+        def _():
+            for g in range(GROUPS):
+                give_back(send_b, recv_b, 1, g)
+
         arrived(recv_b, 1)
         back = recv_b[...]
         mixed = (gate0 * dot(take0[...], back) + gate1 * dot(take1[...], back)).astype(BF)
@@ -295,15 +324,17 @@
             def _():
                 send(g_new, g_in, hs.at[3], hr.at[3], (below, e))
 
-        arrived(recv_c, 2)
-        grads = recv_c[...]
-        for j in range(ffh // part):
-            lo = j * part
-            hg = dot_t(grads, w_o[0, 0, lo : lo + part, :])
-            joined[:, lo : lo + part] = (hg * gate_f[:, lo : lo + part]).astype(BF)
-            joined[:, ffh + lo : ffh + lo + part] = (hg * up_f[:, lo : lo + part]).astype(BF)
-        send_d[...] = dot_t(joined[...], w_gu[0, 0]).astype(BF)
-        exchange(send_d, recv_d, 3)
+        for g in range(GROUPS):
+            group_arrived(recv_c, 2, g)
+            span = slice(g * height, (g + 1) * height)
+            grads = recv_c[span]
+            for j in range(ffh // part):
+                lo = j * part
+                hg = dot_t(grads, w_o[0, 0, lo : lo + part, :])
+                joined[span, lo : lo + part] = (hg * gate_f[span, lo : lo + part]).astype(BF)
+                joined[span, ffh + lo : ffh + lo + part] = (hg * up_f[span, lo : lo + part]).astype(BF)
+            send_d[span] = dot_t(joined[span], w_gu[0, 0]).astype(BF)
+            give_back(send_d, recv_d, 3, g)
         arrived(recv_d, 3)
         back = recv_d[...]
         lg_out[...] = (dot(take0[...], back) + dot(take1[...], back)).astype(BF)
@@ -403,14 +434,14 @@
             dma((5,)), dma((5,)),
             dma((5,)), dma((5,)),
             dma((5,)), dma((5,)),
-            dma((4,)), dma((4,)),
+            dma((4,)), dma((4, GROUPS)),
             dma((5,)), dma((5,)),
             dma((1,)),
         ],
         compiler_params=pltpu.CompilerParams(
             collective_id=0, has_side_effects=True, vmem_limit_bytes=56 * 1024 * 1024
         ),
-    )(tokens, cot, w_down, w_up, w_gu, w_o, routes, gates, counts)
+    )(tokens, cot, w_down, w_up, w_gu, w_o, jnp.swapaxes(routes, 1, 2), jnp.swapaxes(gates, 1, 2), counts)
 
 
 def solution(mesh):

time: 258 us -> 245 us (0.950)
  Pallas kernels: 249 us -> 238 us
  local copies, waits for them, and re-layouts: 6.18 us -> 3.35 us
    pallas_call x1, Pallas kernels: 249 us -> 238 us  [body(): pl.pallas_call(functools.partial(kernel, sections, experts), out_shape=(s...]
    unnamed x6 -> x4, local copies, waits for them, and re-layouts: 6.18 us -> 3.35 us
where the time goes in v2:
time: 245 us; the launch traced here: 243 us
  Pallas kernels  238 us (97%)
  local copies, waits for them, and re-layouts  3.35 us (1%)
    pallas_call x1, Pallas kernels, body(): pl.pallas_call(functools.partial(kernel, sections, experts), out_shape=(s...  238 us

profile of v2, /device:TPU:1, one launch (start us, length us, event | category | flops | bytes accessed | tf_op | source)
XLA Modules:
  0.0 243.1 jit_solution(6595453344077275647)
XLA Ops:
  1.3 238.4 %shard_map.104 = (bf16[1,128,4096]{2,1,0:T(8,128)(2,1)}, bf16[1,128,4096]{2,1,0:T(8,128)(2,1)}) custom-call(bf16[128,4096]{1,0:T(8,128)(2,1)} %tokens.1, bf16[128,4096]{1,0:T(8,128)(2,1)} %cot.1, bf16[1,128,512]{2,1,0:T(8,128)(2,1)} %w_down.1, bf16[1,16,4096]{2,1,0:T(8,128)(2,1)} %w_up.1, bf16[1,1,512,2048]{3,2,1,0:T(8,128)(2,1)} %w_gu.1, ...), custom_call_target="tpu_custom_call" | custom-call | tf_op jit(solution)/shard_map/pallas_call | solution.py:406
  239.7 0.0 copy-start
  239.7 2.4 copy.14
  242.1 0.0 copy-done
  242.1 1.0 copy.15
Async XLA Ops:
  239.7 2.4 copy-start

commit v3 on v2

v3 whole, which is shorter than its diff:
```python
import functools

import jax
import jax.numpy as jnp
from jax import lax
from jax.experimental import pallas as pl
from jax.experimental.pallas import tpu as pltpu
from jax.sharding import PartitionSpec as P

EPS = 1e-05
MESH = pl.DeviceIdType.MESH
BF = jnp.bfloat16
F32 = jnp.float32
SLOT = 16
GROUPS = 2
PER = 32 // GROUPS
ORDER = sorted(
    [(dx, dy, dc) for dx in range(4) for dy in range(4) for dc in range(2) if (dx, dy, dc) != (0, 0, 0)],
    key=lambda k: -(min(k[0], 4 - k[0]) + min(k[1], 4 - k[1])),
)


def dot(a, b):
    return jnp.dot(a, b, preferred_element_type=F32)


def dot_t(a, b):
    return lax.dot_general(a, b, (((1,), (1,)), ((), ())), preferred_element_type=F32)


def kernel(
    sections, experts,
    tokens, cot, w_down, w_up, w_gu, w_o, routes, gates, counts,
    out, gin,
    up_all, down_full, quarter, lat_q,
    x_in, g_in,
    gate_f, up_f, hidden, joined,
    send_a, recv_a, send_b, recv_b, send_c, recv_c, send_d, recv_d,
    put, take0, take1,
    m_all, mixed_in, mixed_out, q_in, q_out, inv_in, inv_out,
    y_f, lat_f, xw_f, inv_f,
    zs, zr, us, ur, ds, dr, fs, fr, as_, ar, ms, mr, qs, qr, gs, gr,
):
    t = lax.axis_index("section")
    e = lax.axis_index("expert")
    x = e // 8
    y = (e // 2) % 4
    c = e % 2
    above = (t + 1) % sections
    below = (t + sections - 1) % sections
    toks, width = tokens.shape
    lat_w = w_down.shape[2]
    ffh = w_o.shape[2]
    last = sections - 1

    def at(xx, yy, cc):
        return (t, (xx * 4 + yy) * 2 + cc)

    def send(src, dst, ssem, rsem, dev):
        pltpu.make_async_remote_copy(
            src_ref=src, dst_ref=dst, send_sem=ssem, recv_sem=rsem, device_id=dev, device_id_type=MESH
        ).start()

    def wait(ref, sem):
        pltpu.make_async_copy(ref, ref, sem).wait()

    def loop(n, fn):
        def step(i, carry):
            fn(i)
            return carry

        lax.fori_loop(0, n, step, 0)

    barrier = pltpu.get_barrier_semaphore()

    @functools.partial(loop, experts - 1)
    def _(k):
        pl.semaphore_signal(barrier, inc=1, device_id=(t, (e + k + 1) % experts), device_id_type=MESH)

    for k in range(1, sections):
        pl.semaphore_signal(barrier, inc=1, device_id=((t + k) % sections, e), device_id_type=MESH)
    pl.semaphore_wait(barrier, experts - 1 + sections - 1)

    def first(buf, ha, hb, ss, rs):
        for d in range(1, 4):
            blk = buf.at[(x, y, c) + ha]
            send(blk, blk, ss.at[0], rs.at[0], at((x + d) % 4, y, c))
            blk = buf.at[(x, y, c) + hb]
            send(blk, blk, ss.at[1], rs.at[1], at(x, (y + d) % 4, c))

    def second(buf, ha, hb, ss, rs):
        wait(buf.at[(pl.ds(0, 3), 0, 0) + ha], rs.at[0])
        wait(buf.at[(pl.ds(0, 3), 0, 0) + hb], rs.at[1])
        for d in range(1, 4):
            blk = buf.at[(slice(None), y, c) + ha]
            send(blk, blk, ss.at[2], rs.at[2], at(x, (y + d) % 4, c))
            blk = buf.at[(x, slice(None), c) + hb]
            send(blk, blk, ss.at[3], rs.at[3], at((x + d) % 4, y, c))

    def third(buf, ha, hb, ss, rs):
        wait(buf.at[(pl.ds(0, 3), slice(None), 0) + ha], rs.at[2])
        wait(buf.at[(pl.ds(0, 3), slice(None), 0) + hb], rs.at[3])
        blk = buf.at[:, :, c]
        send(blk, blk, ss.at[4], rs.at[4], at(x, y, 1 - c))

    def fourth(buf, ha, hb, ss, rs):
        wait(buf.at[:, :, 0], rs.at[4])

    def gather_done(buf, ha, hb, ss, rs):
        wait(buf.at[(pl.ds(0, 3), 0, 0) + ha], ss.at[0])
        wait(buf.at[(pl.ds(0, 3), 0, 0) + hb], ss.at[1])
        wait(buf.at[(pl.ds(0, 3), slice(None), 0) + ha], ss.at[2])
        wait(buf.at[(pl.ds(0, 3), slice(None), 0) + hb], ss.at[3])
        wait(buf.at[:, :, 0], ss.at[4])

    half_cols = width // 2
    half_rows = w_down.shape[1] // 2
    d_a = (pl.ds(0, half_rows), slice(None))
    d_b = (pl.ds(half_rows, half_rows), slice(None))

    def up(i):
        return (
            up_all.at[i],
            (slice(None), pl.ds(0, half_cols)),
            (slice(None), pl.ds(half_cols, half_cols)),
            us.at[i],
            ur.at[i],
        )

    down = (down_full, d_a, d_b, ds, dr)
    piece = (quarter, d_a, d_b, fs, fr)

    lanes = lat_w // sections

    @pl.when(t == 0)
    def _():
        for k in range(1, sections):
            send(w_down.at[0, :, pl.ds(k * lanes, lanes)], quarter.at[x, y, c], zs.at[0], zr.at[0], (k, e))
        quarter[x, y, c] = w_down[0, :, 0:lanes]

    up_all[t, x, y, c] = w_up[0]
    for k in range(1, sections):

        @pl.when(t < k)
        def _():
            send(w_up.at[0], up_all.at[t, x, y, c], zs.at[1], zr.at[1 + t], (k, e))

    @pl.when(t > 0)
    def _():
        wait(quarter.at[0, 0, 0], zr.at[0])

    first(*piece)
    x_in[...] = tokens[...]

    @pl.when(t == last)
    def _():
        g_in[...] = cot[...]

    count = counts[...]
    expert_lane = lax.broadcasted_iota(jnp.int32, (toks, experts), 1)
    live = lax.broadcasted_iota(jnp.int32, (toks, experts), 0) < count

    def column(row):
        return jnp.broadcast_to(row, (toks, toks)).T

    one0 = jnp.where((column(routes[0, 0:1])[:, 0:experts] == expert_lane) & live, 1.0, 0.0).astype(F32)
    one1 = jnp.where((column(routes[0, 1:2])[:, 0:experts] == expert_lane) & live, 1.0, 0.0).astype(F32)
    below_diag = jnp.where(
        lax.broadcasted_iota(jnp.int32, (toks, toks), 0) > lax.broadcasted_iota(jnp.int32, (toks, toks), 1), 1.0, 0.0
    ).astype(BF)
    before = dot(below_diag, (one0 + one1).astype(BF))
    slots = experts * SLOT
    spread = jnp.where(
        lax.broadcasted_iota(jnp.int32, (experts, slots), 1) // SLOT
        == lax.broadcasted_iota(jnp.int32, (experts, slots), 0),
        1.0,
        0.0,
    ).astype(BF)
    slot_no = (lax.broadcasted_iota(jnp.int32, (toks, slots), 1) % SLOT).astype(F32)
    here = dot(before.astype(BF), spread) == slot_no
    pick0 = jnp.where(here, dot(one0.astype(BF), spread), 0.0)
    pick1 = jnp.where(here, dot(one1.astype(BF), spread), 0.0)
    take0[...] = pick0.astype(BF)
    take1[...] = pick1.astype(BF)
    put[:, 0:toks] = pick0.T.astype(BF)
    put[:, toks : 2 * toks] = pick1.T.astype(BF)
    gate0 = column(gates[0, 0:1])[:, 0:1]
    gate1 = column(gates[0, 1:2])[:, 0:1]

    second(*piece)
    chunk = 512
    n_chunks = width // chunk

    def cols_of(j):
        return slice(j * chunk, (j + 1) * chunk)

    def up_chunk(i, j):
        return up_all[i, :, :, :, :, j * chunk : (j + 1) * chunk].reshape(lat_w, chunk)

    def down_chunk(buf, j):
        return buf[j // 2, 2 * (j % 2) : 2 * (j % 2) + 2].reshape(chunk, buf.shape[-1])

    def inv_rms(square):
        return lax.rsqrt(square / width + EPS)

    square = jnp.zeros((toks, 1), F32)
    for j in range(n_chunks):
        wide = tokens[:, cols_of(j)].astype(F32)
        square += jnp.sum(wide * wide, axis=1, keepdims=True)
    inv_f[...] = jnp.broadcast_to(inv_rms(square), inv_f.shape)
    third(*piece)
    fourth(*piece)
    total = jnp.zeros((toks, lanes), F32)
    for j in range(n_chunks):
        total += dot(tokens[:, cols_of(j)], down_chunk(quarter, j))
    lat_q[t] = (total * inv_f[...]).astype(BF)

    @pl.when(t > 0)
    def _():
        send(lat_q.at[t], lat_q.at[t], zs.at[2], zr.at[5], (0, e))

    first(*up(t))

    def product(i):
        m_all[i] = dot(up_all[i].reshape(lat_w, width), down_full[...].reshape(width, lat_w)).astype(BF)

    @pl.when(t > 0)
    def _():
        down_full[x, y, c] = w_down[0]
        first(*down)

        @functools.partial(loop, t)
        def _(i):
            wait(w_up.at[0], zr.at[1 + i])
            first(*up(i))

        second(*down)
        loop(t, lambda i: second(*up(i)))
        third(*down)
        loop(t, lambda i: third(*up(i)))
        second(*up(t))
        fourth(*down)
        loop(t, lambda i: fourth(*up(i)))
        loop(t, product)

    def block(i):
        return pl.ds(pl.multiple_of(i * SLOT, SLOT), SLOT)

    def dispatch(src, dst, k):
        for pos, (dx, dy, dc) in enumerate(ORDER):
            p = (((x + dx) % 4) * 4 + (y + dy) % 4) * 2 + (c + dc) % 2
            send(src.at[block(p)], dst.at[block(pos)], as_.at[k], ar.at[k, pos // PER], (t, p))
        dst[block(experts - 1)] = src[block(e)]

    def give_back(src, dst, k, g):
        for pos, (dx, dy, dc) in enumerate(ORDER):
            if pos // PER == g:
                p = (((x + 4 - dx) % 4) * 4 + (y + 4 - dy) % 4) * 2 + (c + dc) % 2
                send(src.at[block(pos)], dst.at[block(e)], as_.at[k], ar.at[k, 0], (t, p))
        if g == GROUPS - 1:
            dst[block(e)] = src[block(experts - 1)]

    def group_arrived(buf, k, g):
        size = PER if g < GROUPS - 1 else PER - 1
        wait(buf.at[pl.ds(0, size * SLOT)], ar.at[k, g])

    def arrived(buf, k):
        wait(buf.at[pl.ds(0, (experts - 1) * SLOT)], ar.at[k, 0])

    def route_grads():
        mg = q_in[t].astype(F32)
        both = jnp.concatenate([(gate0 * mg).astype(BF), (gate1 * mg).astype(BF)], axis=0)
        send_c[...] = dot(put[...], both).astype(BF)
        dispatch(send_c, recv_c, 2)

    def back_through(ref, i):
        total = jnp.zeros((toks, lat_w), F32)
        for j in range(n_chunks):
            total += dot_t(ref[:, cols_of(j)], up_chunk(i, j))
        return total

    @pl.when(t == last)
    def _():
        third(*up(t))
        fourth(*up(t))

        @functools.partial(loop, sections)
        def _(i):
            q_in[i] = back_through(cot, i).astype(BF)

        route_grads()

    def add_mixed(i):
        for j in range(n_chunks):
            new = x_in[:, cols_of(j)].astype(F32) + dot(mixed_in[i], up_chunk(i, j))
            x_in[:, cols_of(j)] = new.astype(BF)

    def pass_on(i):
        @pl.when(t < last)
        def _():
            send(mixed_in.at[i], mixed_in.at[i], ms.at[i], mr.at[i], (above, e))

    @functools.partial(loop, t - 1)
    def _(i):
        wait(mixed_in.at[i], mr.at[i])
        pass_on(i)
        add_mixed(i)

    @pl.when(t > 0)
    def _():
        total = jnp.zeros((toks, lat_w), F32)
        for j in range(n_chunks):
            total += dot(x_in[:, cols_of(j)], down_chunk(down_full, j))
        y_f[...] = total

    @pl.when(t == 0)
    def _():
        wait(lat_q.at[pl.ds(0, sections - 1)], zr.at[5])
        lat_f[...] = jnp.concatenate([lat_q[k] for k in range(sections)], axis=1).astype(F32)

    @pl.when(t > 0)
    def _():
        wait(mixed_in.at[t - 1], mr.at[t - 1])
        raw = y_f[...] + dot(mixed_in[t - 1], m_all[t - 1])
        wait(inv_in, zr.at[6])
        inv = column(inv_in[0:1])
        inv_f[...] = inv
        lat_f[...] = raw * inv[:, 0:1]

    lat = lat_f[...].astype(BF)
    send_a[...] = dot(put[...], jnp.concatenate([lat, lat], axis=0)).astype(BF)
    dispatch(send_a, recv_a, 0)

    @pl.when(t == 0)
    def _():
        second(*up(t))

    @pl.when(t > 0)
    def _():
        pass_on(t - 1)
        add_mixed(t - 1)
        xw_f[...] = back_through(x_in, t - 1)

    part = 256
    height = PER * SLOT
    for g in range(GROUPS):
        group_arrived(recv_a, 0, g)
        span = slice(g * height, (g + 1) * height)
        rows = recv_a[span]
        for j in range(ffh // part):
            lo = j * part
            a = dot(rows, w_gu[0, 0, :, lo : lo + part])
            u = dot(rows, w_gu[0, 0, :, ffh + lo : ffh + lo + part])
            sig = 1.0 / (1.0 + jnp.exp(-a))
            silu = a * sig
            hidden[span, lo : lo + part] = (silu * u).astype(BF)
            up_f[span, lo : lo + part] = silu
            gate_f[span, lo : lo + part] = u * sig * (1.0 + a * (1.0 - sig))
        send_b[span] = dot(hidden[span], w_o[0, 0]).astype(BF)

        @pl.when(t < last)
        def _():
            give_back(send_b, recv_b, 1, g)

    def forward_finish():
        @pl.when(t == last)
        def _():
            for g in range(GROUPS):
                give_back(send_b, recv_b, 1, g)

        @pl.when(t < last)
        def _():
            third(*up(t))
            fourth(*up(t))

        arrived(recv_b, 1)
        back = recv_b[...]
        mixed = (gate0 * dot(take0[...], back) + gate1 * dot(take1[...], back)).astype(BF)
        mixed_out[...] = mixed

        @pl.when(t < last)
        def _():
            send(mixed_out, mixed_in.at[t], ms.at[t], mr.at[t], (above, e))

        square = jnp.zeros((toks, 1), F32)
        for j in range(n_chunks):
            new = (x_in[:, cols_of(j)].astype(F32) + dot(mixed, up_chunk(t, j))).astype(BF)
            out[0, :, cols_of(j)] = new
            wide = new.astype(F32)
            square += jnp.sum(wide * wide, axis=1, keepdims=True)

        @pl.when(t < last)
        def _():
            inv_out[...] = jnp.broadcast_to(inv_rms(square), (toks, toks)).T[0 : inv_out.shape[0]]
            send(inv_out, inv_in, zs.at[3], zr.at[6], (above, e))

        @pl.when(t == 0)
        def _():
            down_full[x, y, c] = w_down[0]
            for phase in (first, second, third, fourth):
                phase(*down)

    wide_chunk = width // 4

    def backward():
        @pl.when(t < last)
        def _():
            wait(q_in.at[t], qr.at[t])
            route_grads()

        for g in range(GROUPS):
            group_arrived(recv_c, 2, g)
            span = slice(g * height, (g + 1) * height)
            grads = recv_c[span]
            for j in range(ffh // part):
                lo = j * part
                hg = dot_t(grads, w_o[0, 0, lo : lo + part, :])
                joined[span, lo : lo + part] = (hg * gate_f[span, lo : lo + part]).astype(BF)
                joined[span, ffh + lo : ffh + lo + part] = (hg * up_f[span, lo : lo + part]).astype(BF)
            send_d[span] = dot_t(joined[span], w_gu[0, 0]).astype(BF)
            give_back(send_d, recv_d, 3, g)

        arrived(recv_d, 3)
        back = recv_d[...]
        lg = (dot(take0[...], back) + dot(take1[...], back)).astype(BF)
        inv = inv_f[:, 0:1]
        dotted = jnp.sum(lg.astype(F32) * lat_f[...], axis=1, keepdims=True) / width
        scale = inv * inv * dotted

        def mix_grad(i, xw):
            q_out[i] = (q_in[i].astype(F32) + inv * dot_t(lg, m_all[i]) - scale * xw).astype(BF)
            send(q_out.at[i], q_in.at[i], qs.at[i], qr.at[i], (below, e))

        @pl.when(t > 0)
        def _():
            @pl.when(t < last)
            def _():
                loop(t, lambda i: wait(q_in.at[i], qr.at[i]))

            mix_grad(t - 1, xw_f[...])

        for j in range(4):
            here = pl.ds(j * wide_chunk, wide_chunk)

            @pl.when(t < last)
            def _():
                wait(g_in.at[:, here], gr.at[j])

            for h in range(2 * j, 2 * j + 2):
                ng = dot_t(lg, down_chunk(down_full, h))
                new = g_in[:, cols_of(h)].astype(F32) + inv * ng - scale * x_in[:, cols_of(h)].astype(F32)
                gin[0, :, cols_of(h)] = new.astype(BF)

            @pl.when(t > 0)
            def _():
                send(gin.at[0, :, here], g_in.at[:, here], gs.at[j], gr.at[j], (below, e))

        loop(t - 1, lambda i: mix_grad(i, back_through(x_in, i)))

    def stage(i):
        @pl.when((i == 0) == (t == last))
        def _():
            backward()

        @pl.when(i == 0)
        def _():
            forward_finish()

    loop(2, stage)

    @pl.when(t == 0)
    def _():
        wait(lat_q.at[pl.ds(0, sections - 1)], zs.at[0])

    @pl.when(t > 0)
    def _():
        wait(lat_q.at[0], zs.at[2])

    loop(last - t, lambda i: wait(w_up.at[0], zs.at[1]))
    gather_done(*piece)
    gather_done(*down)
    loop(t + 1, lambda i: gather_done(*up(i)))
    for k in range(4):
        wait(recv_a.at[pl.ds(0, (experts - 1) * SLOT)], as_.at[k])

    @pl.when(t < last)
    def _():
        loop(t + 1, lambda i: wait(mixed_out, ms.at[i]))
        wait(inv_out, zs.at[3])

    @pl.when(t > 0)
    def _():
        loop(t, lambda i: wait(mixed_out, qs.at[i]))
        for j in range(4):
            wait(g_in.at[:, pl.ds(0, wide_chunk)], gs.at[j])


def body(sections, experts, tokens, cot, w_down, w_up, w_gu, w_o, routes, gates, counts):
    toks, width = tokens.shape
    lat_w = w_down.shape[2]
    ffh = w_o.shape[2]
    slots = experts * SLOT
    vm = pltpu.VMEM
    dma = pltpu.SemaphoreType.DMA
    rows = [vm((slots, lat_w), BF) for _ in range(8)]
    spec = pl.BlockSpec(memory_space=pltpu.VMEM)
    shape = jax.ShapeDtypeStruct((1, toks, width), BF)
    return pl.pallas_call(
        functools.partial(kernel, sections, experts),
        out_shape=(shape, shape),
        in_specs=[spec] * 9,
        out_specs=(spec, spec),
        scratch_shapes=[
            vm((sections, 4, 4, 2, lat_w // experts, width), BF),
            vm((4, 4, 2, width // experts, lat_w), BF),
            vm((4, 4, 2, width // experts, lat_w // sections), BF),
            vm((sections, toks, lat_w // sections), BF),
            vm((toks, width), BF),
            vm((toks, width), BF),
            vm((slots, ffh), F32),
            vm((slots, ffh), F32),
            vm((slots, ffh), BF),
            vm((slots, 2 * ffh), BF),
            *rows,
            vm((slots, 2 * toks), BF),
            vm((toks, slots), BF),
            vm((toks, slots), BF),
            vm((sections - 1, lat_w, lat_w), BF),
            vm((sections - 1, toks, lat_w), BF),
            vm((toks, lat_w), BF),
            vm((sections, toks, lat_w), BF),
            vm((sections - 1, toks, lat_w), BF),
            vm((8, toks), F32),
            vm((8, toks), F32),
            vm((toks, lat_w), F32),
            vm((toks, lat_w), F32),
            vm((toks, lat_w), F32),
            vm((toks, 128), F32),
            dma((4,)), dma((7,)),
            dma((sections, 5)), dma((sections, 5)),
            dma((5,)), dma((5,)),
            dma((5,)), dma((5,)),
            dma((4,)), dma((4, GROUPS)),
            dma((sections,)), dma((sections,)),
            dma((sections,)), dma((sections,)),
            dma((4,)), dma((4,)),
        ],
        compiler_params=pltpu.CompilerParams(
            collective_id=0, has_side_effects=True, vmem_limit_bytes=60 * 1024 * 1024
        ),
    )(
        tokens, cot, w_down, w_up, w_gu, w_o, jnp.swapaxes(routes, 1, 2), jnp.swapaxes(gates, 1, 2), counts
    )


def solution(mesh):
    in_specs = (
        P("expert", None),
        P("expert", None),
        P("section", "expert", None),
        P("section", "expert", None),
        P("section", "expert", None, None),
        P("section", "expert", None, None),
        P("section", "expert", None),
        P("section", "expert", None),
        P("section", "expert"),
    )
    out_specs = (P("section", "expert", None), P("section", "expert", None))
    step = functools.partial(body, mesh.shape["section"], mesh.shape["expert"])
    return jax.shard_map(step, mesh=mesh, in_specs=in_specs, out_specs=out_specs, check_vma=False)
```

time: 245 us -> 234 us (0.955)
  Pallas kernels: 238 us -> 228 us
    pallas_call x1, Pallas kernels: 238 us -> 228 us  [body(): pl.pallas_call(functools.partial(kernel, sections, experts), out_shape=(s...]
where the time goes in v3:
time: 234 us; the launch traced here: 233 us
  Pallas kernels  228 us (97%)
  local copies, waits for them, and re-layouts  3.35 us (1%)
    pallas_call x1, Pallas kernels, body(): pl.pallas_call(functools.partial(kernel, sections, experts), out_shape=(s...  228 us

profile of v3, /device:TPU:1, one launch (start us, length us, event | category | flops | bytes accessed | tf_op | source)
XLA Modules:
  0.0 233.0 jit_solution(14213793316741941805)
XLA Ops:
  1.3 228.3 %shard_map.104 = (bf16[1,128,4096]{2,1,0:T(8,128)(2,1)}, bf16[1,128,4096]{2,1,0:T(8,128)(2,1)}) custom-call(bf16[128,4096]{1,0:T(8,128)(2,1)} %tokens.1, bf16[128,4096]{1,0:T(8,128)(2,1)} %cot.1, bf16[1,128,512]{2,1,0:T(8,128)(2,1)} %w_down.1, bf16[1,16,4096]{2,1,0:T(8,128)(2,1)} %w_up.1, bf16[1,1,512,2048]{3,2,1,0:T(8,128)(2,1)} %w_gu.1, ...), custom_call_target="tpu_custom_call" | custom-call | tf_op jit(solution)/shard_map/pallas_call | solution.py:508
  229.6 0.0 copy-start
  229.6 2.4 %copy.14 = bf16[1,128,4096]{2,1,0:T(8,128)(2,1)} copy(bf16[1,128,4096]{2,1,0:T(8,128)(2,1)} %get-tuple-element.4) | data formatting | bytes 2097152
  232.0 0.0 copy-done
  232.0 1.0 copy.15
Async XLA Ops:
  229.6 2.4 %copy-start = (bf16[1,128,4096]{2,1,0:T(8,128)(2,1)S(1)}, bf16[1,128,4096]{2,1,0:T(8,128)(2,1)}, u32[]{:S(2)}) copy-start(bf16[1,128,4096]{2,1,0:T(8,128)(2,1)} %get-tuple-element.5) | copy-start | bytes 3145732

commit v4 on v3

--- a/solution.py
+++ b/solution.py
@@ -37,7 +37,7 @@
     gate_f, up_f, hidden, joined,
     send_a, recv_a, send_b, recv_b, send_c, recv_c, send_d, recv_d,
     put, take0, take1,
-    m_all, mixed_in, mixed_out, q_in, q_out, inv_in, inv_out,
+    m_all, mixed_in, mixed_out, q_in, q_out,
     y_f, lat_f, xw_f, inv_f,
     zs, zr, us, ur, ds, dr, fs, fr, as_, ar, ms, mr, qs, qr, gs, gr,
 ):
@@ -128,15 +128,19 @@
         )
 
     down = (down_full, d_a, d_b, ds, dr)
-    piece = (quarter, d_a, d_b, fs, fr)
+    piece = (quarter.at[0], d_a, d_b, fs.at[0], fr.at[0])
+    piece2 = (quarter.at[1], d_a, d_b, fs.at[1], fr.at[1])
 
     lanes = lat_w // sections
 
     @pl.when(t == 0)
     def _():
-        for k in range(1, sections):
-            send(w_down.at[0, :, pl.ds(k * lanes, lanes)], quarter.at[x, y, c], zs.at[0], zr.at[0], (k, e))
-        quarter[x, y, c] = w_down[0, :, 0:lanes]
+        for k in range(2, sections):
+            send(w_down.at[0, :, pl.ds(k * lanes, lanes)], quarter.at[0, x, y, c], zs.at[0], zr.at[0], (k, e))
+        quarter[0, x, y, c] = w_down[0, :, 0:lanes]
+        quarter[1, x, y, c] = w_down[0, :, lanes : 2 * lanes]
+        first(*piece)
+        first(*piece2)
 
     up_all[t, x, y, c] = w_up[0]
     for k in range(1, sections):
@@ -145,11 +149,31 @@
         def _():
             send(w_up.at[0], up_all.at[t, x, y, c], zs.at[1], zr.at[1 + t], (k, e))
 
-    @pl.when(t > 0)
-    def _():
-        wait(quarter.at[0, 0, 0], zr.at[0])
-
-    first(*piece)
+    @pl.when(t == last)
+    def _():
+        send(w_up.at[0], up_all.at[t, x, y, c], zs.at[1], zr.at[1 + t], (0, e))
+
+    @pl.when(t > 1)
+    def _():
+        wait(quarter.at[0, 0, 0, 0], zr.at[0])
+        first(*piece)
+
+    def product(i):
+        m_all[i] = dot(up_all[i].reshape(lat_w, width), down_full[...].reshape(width, lat_w)).astype(BF)
+
+    def gather_first():
+        down_full[x, y, c] = w_down[0]
+        first(*down)
+
+        @functools.partial(loop, t)
+        def _(i):
+            wait(w_up.at[0], zr.at[1 + i])
+            first(*up(i))
+
+    @pl.when(t == 1)
+    def _():
+        gather_first()
+
     x_in[...] = tokens[...]
 
     @pl.when(t == last)
@@ -187,7 +211,14 @@
     gate0 = column(gates[0, 0:1])[:, 0:1]
     gate1 = column(gates[0, 1:2])[:, 0:1]
 
-    second(*piece)
+    @pl.when(t != 1)
+    def _():
+        second(*piece)
+
+    @pl.when(t == 0)
+    def _():
+        second(*piece2)
+
     chunk = 512
     n_chunks = width // chunk
 
@@ -208,40 +239,41 @@
         wide = tokens[:, cols_of(j)].astype(F32)
         square += jnp.sum(wide * wide, axis=1, keepdims=True)
     inv_f[...] = jnp.broadcast_to(inv_rms(square), inv_f.shape)
-    third(*piece)
-    fourth(*piece)
-    total = jnp.zeros((toks, lanes), F32)
-    for j in range(n_chunks):
-        total += dot(tokens[:, cols_of(j)], down_chunk(quarter, j))
-    lat_q[t] = (total * inv_f[...]).astype(BF)
+    def raw_piece(k):
+        total = jnp.zeros((toks, lanes), F32)
+        for j in range(n_chunks):
+            total += dot(tokens[:, cols_of(j)], down_chunk(quarter.at[k], j))
+        return (total * inv_f[...]).astype(BF)
+
+    @pl.when(t != 1)
+    def _():
+        third(*piece)
+
+    @pl.when(t == 0)
+    def _():
+        third(*piece2)
+        fourth(*piece2)
+        lat_q[1] = raw_piece(1)
+
+    @pl.when(t != 1)
+    def _():
+        fourth(*piece)
+        lat_q[t] = raw_piece(0)
+
+    @pl.when(t > 1)
+    def _():
+        send(lat_q.at[t], lat_q.at[t], zs.at[2], zr.at[5], (0, e))
+        gather_first()
 
     @pl.when(t > 0)
     def _():
-        send(lat_q.at[t], lat_q.at[t], zs.at[2], zr.at[5], (0, e))
-
-    first(*up(t))
-
-    def product(i):
-        m_all[i] = dot(up_all[i].reshape(lat_w, width), down_full[...].reshape(width, lat_w)).astype(BF)
-
-    @pl.when(t > 0)
-    def _():
-        down_full[x, y, c] = w_down[0]
-        first(*down)
-
-        @functools.partial(loop, t)
-        def _(i):
-            wait(w_up.at[0], zr.at[1 + i])
-            first(*up(i))
-
         second(*down)
         loop(t, lambda i: second(*up(i)))
         third(*down)
         loop(t, lambda i: third(*up(i)))
-        second(*up(t))
         fourth(*down)
         loop(t, lambda i: fourth(*up(i)))
-        loop(t, product)
+        product(t - 1)
 
     def block(i):
         return pl.ds(pl.multiple_of(i * SLOT, SLOT), SLOT)
@@ -281,19 +313,17 @@
 
     @pl.when(t == last)
     def _():
-        third(*up(t))
-        fourth(*up(t))
-
-        @functools.partial(loop, sections)
-        def _(i):
-            q_in[i] = back_through(cot, i).astype(BF)
-
+        wait(q_in.at[t], qr.at[t])
         route_grads()
 
     def add_mixed(i):
+        square = jnp.zeros((toks, 1), F32)
         for j in range(n_chunks):
-            new = x_in[:, cols_of(j)].astype(F32) + dot(mixed_in[i], up_chunk(i, j))
-            x_in[:, cols_of(j)] = new.astype(BF)
+            new = (x_in[:, cols_of(j)].astype(F32) + dot(mixed_in[i], up_chunk(i, j))).astype(BF)
+            x_in[:, cols_of(j)] = new
+            wide = new.astype(F32)
+            square += jnp.sum(wide * wide, axis=1, keepdims=True)
+        return square
 
     def pass_on(i):
         @pl.when(t < last)
@@ -315,31 +345,28 @@
 
     @pl.when(t == 0)
     def _():
-        wait(lat_q.at[pl.ds(0, sections - 1)], zr.at[5])
+        wait(lat_q.at[pl.ds(0, sections - 2)], zr.at[5])
         lat_f[...] = jnp.concatenate([lat_q[k] for k in range(sections)], axis=1).astype(F32)
 
     @pl.when(t > 0)
     def _():
         wait(mixed_in.at[t - 1], mr.at[t - 1])
-        raw = y_f[...] + dot(mixed_in[t - 1], m_all[t - 1])
-        wait(inv_in, zr.at[6])
-        inv = column(inv_in[0:1])
-        inv_f[...] = inv
-        lat_f[...] = raw * inv[:, 0:1]
+        pass_on(t - 1)
+        inv = inv_rms(add_mixed(t - 1))
+        inv_f[...] = jnp.broadcast_to(inv, inv_f.shape)
+        lat_f[...] = (y_f[...] + dot(mixed_in[t - 1], m_all[t - 1])) * inv
 
     lat = lat_f[...].astype(BF)
     send_a[...] = dot(put[...], jnp.concatenate([lat, lat], axis=0)).astype(BF)
     dispatch(send_a, recv_a, 0)
 
-    @pl.when(t == 0)
-    def _():
-        second(*up(t))
-
     @pl.when(t > 0)
     def _():
-        pass_on(t - 1)
-        add_mixed(t - 1)
         xw_f[...] = back_through(x_in, t - 1)
+
+    @pl.when(t == last)
+    def _():
+        q_in[t - 1] = back_through(cot, t - 1).astype(BF)
 
     part = 256
     height = PER * SLOT
@@ -368,11 +395,6 @@
             for g in range(GROUPS):
                 give_back(send_b, recv_b, 1, g)
 
-        @pl.when(t < last)
-        def _():
-            third(*up(t))
-            fourth(*up(t))
-
         arrived(recv_b, 1)
         back = recv_b[...]
         mixed = (gate0 * dot(take0[...], back) + gate1 * dot(take1[...], back)).astype(BF)
@@ -382,17 +404,20 @@
         def _():
             send(mixed_out, mixed_in.at[t], ms.at[t], mr.at[t], (above, e))
 
-        square = jnp.zeros((toks, 1), F32)
+        @pl.when(t == 0)
+        def _():
+            wait(w_up.at[0], zr.at[1 + last])
+            for phase in (first, second, third, fourth):
+                phase(*up(last))
+            q_out[0] = back_through(cot, last).astype(BF)
+            send(q_out.at[0], q_in.at[last], qs.at[0], qr.at[last], (last, e))
+
+        for phase in (first, second, third, fourth):
+            phase(*up(t))
+
         for j in range(n_chunks):
-            new = (x_in[:, cols_of(j)].astype(F32) + dot(mixed, up_chunk(t, j))).astype(BF)
-            out[0, :, cols_of(j)] = new
-            wide = new.astype(F32)
-            square += jnp.sum(wide * wide, axis=1, keepdims=True)
-
-        @pl.when(t < last)
-        def _():
-            inv_out[...] = jnp.broadcast_to(inv_rms(square), (toks, toks)).T[0 : inv_out.shape[0]]
-            send(inv_out, inv_in, zs.at[3], zr.at[6], (above, e))
+            new = x_in[:, cols_of(j)].astype(F32) + dot(mixed_out[...], up_chunk(t, j))
+            out[0, :, cols_of(j)] = new.astype(BF)
 
         @pl.when(t == 0)
         def _():
@@ -428,16 +453,26 @@
         scale = inv * inv * dotted
 
         def mix_grad(i, xw):
+            @pl.when(t < last)
+            def _():
+                wait(q_in.at[i], qr.at[i])
+
             q_out[i] = (q_in[i].astype(F32) + inv * dot_t(lg, m_all[i]) - scale * xw).astype(BF)
             send(q_out.at[i], q_in.at[i], qs.at[i], qr.at[i], (below, e))
 
         @pl.when(t > 0)
         def _():
-            @pl.when(t < last)
-            def _():
-                loop(t, lambda i: wait(q_in.at[i], qr.at[i]))
-
             mix_grad(t - 1, xw_f[...])
+
+            @functools.partial(loop, t - 1)
+            def _(i):
+                product(i)
+
+                @pl.when(t == last)
+                def _():
+                    q_in[i] = back_through(cot, i).astype(BF)
+
+                mix_grad(i, back_through(x_in, i))
 
         for j in range(4):
             here = pl.ds(j * wide_chunk, wide_chunk)
@@ -455,8 +490,6 @@
             def _():
                 send(gin.at[0, :, here], g_in.at[:, here], gs.at[j], gr.at[j], (below, e))
 
-        loop(t - 1, lambda i: mix_grad(i, back_through(x_in, i)))
-
     def stage(i):
         @pl.when((i == 0) == (t == last))
         def _():
@@ -470,14 +503,20 @@
 
     @pl.when(t == 0)
     def _():
-        wait(lat_q.at[pl.ds(0, sections - 1)], zs.at[0])
-
-    @pl.when(t > 0)
+        wait(lat_q.at[pl.ds(0, sections - 2)], zs.at[0])
+        gather_done(*piece2)
+        gather_done(*up(last))
+        wait(q_out.at[0], qs.at[0])
+
+    @pl.when(t > 1)
     def _():
         wait(lat_q.at[0], zs.at[2])
 
-    loop(last - t, lambda i: wait(w_up.at[0], zs.at[1]))
-    gather_done(*piece)
+    @pl.when(t != 1)
+    def _():
+        gather_done(*piece)
+
+    loop(jnp.where(t == last, 1, last - t), lambda i: wait(w_up.at[0], zs.at[1]))
     gather_done(*down)
     loop(t + 1, lambda i: gather_done(*up(i)))
     for k in range(4):
@@ -486,7 +525,6 @@
     @pl.when(t < last)
     def _():
         loop(t + 1, lambda i: wait(mixed_out, ms.at[i]))
-        wait(inv_out, zs.at[3])
 
     @pl.when(t > 0)
     def _():
@@ -513,7 +551,7 @@
         scratch_shapes=[
             vm((sections, 4, 4, 2, lat_w // experts, width), BF),
             vm((4, 4, 2, width // experts, lat_w), BF),
-            vm((4, 4, 2, width // experts, lat_w // sections), BF),
+            vm((2, 4, 4, 2, width // experts, lat_w // sections), BF),
             vm((sections, toks, lat_w // sections), BF),
             vm((toks, width), BF),
             vm((toks, width), BF),
@@ -530,8 +568,6 @@
             vm((toks, lat_w), BF),
             vm((sections, toks, lat_w), BF),
             vm((sections - 1, toks, lat_w), BF),
-            vm((8, toks), F32),
-            vm((8, toks), F32),
             vm((toks, lat_w), F32),
             vm((toks, lat_w), F32),
             vm((toks, lat_w), F32),
@@ -539,7 +575,7 @@
             dma((4,)), dma((7,)),
             dma((sections, 5)), dma((sections, 5)),
             dma((5,)), dma((5,)),
-            dma((5,)), dma((5,)),
+            dma((2, 5)), dma((2, 5)),
             dma((4,)), dma((4, GROUPS)),
             dma((sections,)), dma((sections,)),
             dma((sections,)), dma((sections,)),

time: 234 us -> 201 us (0.86)
  Pallas kernels: 228 us -> 196 us
    pallas_call x1, Pallas kernels: 228 us -> 196 us  [body(): pl.pallas_call(functools.partial(kernel, sections, experts), out_shape=(s...]
where the time goes in v4:
time: 201 us; the launch traced here: 200 us
  Pallas kernels  196 us (98%)
  local copies, waits for them, and re-layouts  3.35 us (2%)
    pallas_call x1, Pallas kernels, body(): pl.pallas_call(functools.partial(kernel, sections, experts), out_shape=(s...  196 us

profile of v4, /device:TPU:1, one launch (start us, length us, event | category | flops | bytes accessed | tf_op | source)
XLA Modules:
  0.0 200.5 jit_solution(2418841681864824710)
XLA Ops:
  1.3 195.8 %shard_map.104 = (bf16[1,128,4096]{2,1,0:T(8,128)(2,1)}, bf16[1,128,4096]{2,1,0:T(8,128)(2,1)}) custom-call(bf16[128,4096]{1,0:T(8,128)(2,1)} %tokens.1, bf16[128,4096]{1,0:T(8,128)(2,1)} %cot.1, bf16[1,128,512]{2,1,0:T(8,128)(2,1)} %w_down.1, bf16[1,16,4096]{2,1,0:T(8,128)(2,1)} %w_up.1, bf16[1,1,512,2048]{3,2,1,0:T(8,128)(2,1)} %w_gu.1, ...), custom_call_target="tpu_custom_call" | custom-call | tf_op jit(solution)/shard_map/pallas_call | solution.py:546
  197.1 0.0 copy-start
  197.1 2.4 %copy.14 = bf16[1,128,4096]{2,1,0:T(8,128)(2,1)} copy(bf16[1,128,4096]{2,1,0:T(8,128)(2,1)} %get-tuple-element.4) | data formatting | bytes 2097152
  199.5 0.0 copy-done
  199.5 1.0 copy.15
Async XLA Ops:
  197.1 2.4 %copy-start = (bf16[1,128,4096]{2,1,0:T(8,128)(2,1)S(1)}, bf16[1,128,4096]{2,1,0:T(8,128)(2,1)}, u32[]{:S(2)}) copy-start(bf16[1,128,4096]{2,1,0:T(8,128)(2,1)} %get-tuple-element.5) | copy-start | bytes 3145732

commit v5 on v4

--- a/solution.py
+++ b/solution.py
@@ -26,6 +26,30 @@
 
 def dot_t(a, b):
     return lax.dot_general(a, b, (((1,), (1,)), ((), ())), preferred_element_type=F32)
+
+
+def swap(v):
+    return jnp.concatenate([v[:, 4:8], v[:, 0:4]], axis=1)
+
+
+def pack(rows):
+    n, w = rows.shape[0] // SLOT, rows.shape[1] // 4
+    full = rows.reshape(n, SLOT, 4 * w)
+    lo, hi = full[:, 0:8], full[:, 8:16]
+    used = lax.broadcasted_iota(jnp.int32, (n, 8, w), 1) < 4
+    tail_lo, tail_hi = lo[:, :, 3 * w :], hi[:, :, 3 * w :]
+    spare = [swap(tail_lo), tail_lo, swap(tail_hi)]
+    hi = jnp.concatenate([jnp.where(used, hi[:, :, k * w : (k + 1) * w], spare[k]) for k in range(3)], axis=2)
+    return jnp.concatenate([lo[:, :, 0 : 3 * w], hi], axis=1).reshape(n * SLOT, 3 * w).astype(BF)
+
+
+def unpack(slabs):
+    n, w = slabs.shape[0] // SLOT, slabs.shape[1] // 3
+    hi = slabs.astype(F32).reshape(n, SLOT, 3 * w)[:, 8:16]
+    used = lax.broadcasted_iota(jnp.int32, (n, 8, w), 1) < 4
+    tail_lo = jnp.where(used, swap(hi[:, :, 0:w]), hi[:, :, w : 2 * w])
+    tail = jnp.concatenate([tail_lo, swap(hi[:, :, 2 * w :])], axis=1).reshape(n * SLOT, w)
+    return jnp.concatenate([slabs, tail.astype(BF)], axis=1)
 
 
 def kernel(
@@ -302,7 +326,7 @@
     def route_grads():
         mg = q_in[t].astype(F32)
         both = jnp.concatenate([(gate0 * mg).astype(BF), (gate1 * mg).astype(BF)], axis=0)
-        send_c[...] = dot(put[...], both).astype(BF)
+        send_c[...] = pack(dot(put[...], both))
         dispatch(send_c, recv_c, 2)
 
     def back_through(ref, i):
@@ -357,7 +381,7 @@
         lat_f[...] = (y_f[...] + dot(mixed_in[t - 1], m_all[t - 1])) * inv
 
     lat = lat_f[...].astype(BF)
-    send_a[...] = dot(put[...], jnp.concatenate([lat, lat], axis=0)).astype(BF)
+    send_a[...] = pack(dot(put[...], jnp.concatenate([lat, lat], axis=0)))
     dispatch(send_a, recv_a, 0)
 
     @pl.when(t > 0)
@@ -373,7 +397,7 @@
     for g in range(GROUPS):
         group_arrived(recv_a, 0, g)
         span = slice(g * height, (g + 1) * height)
-        rows = recv_a[span]
+        rows = unpack(recv_a[span])
         for j in range(ffh // part):
             lo = j * part
             a = dot(rows, w_gu[0, 0, :, lo : lo + part])
@@ -383,7 +407,7 @@
             hidden[span, lo : lo + part] = (silu * u).astype(BF)
             up_f[span, lo : lo + part] = silu
             gate_f[span, lo : lo + part] = u * sig * (1.0 + a * (1.0 - sig))
-        send_b[span] = dot(hidden[span], w_o[0, 0]).astype(BF)
+        send_b[span] = pack(dot(hidden[span], w_o[0, 0]))
 
         @pl.when(t < last)
         def _():
@@ -396,7 +420,7 @@
                 give_back(send_b, recv_b, 1, g)
 
         arrived(recv_b, 1)
-        back = recv_b[...]
+        back = unpack(recv_b[...])
         mixed = (gate0 * dot(take0[...], back) + gate1 * dot(take1[...], back)).astype(BF)
         mixed_out[...] = mixed
 
@@ -436,17 +460,17 @@
         for g in range(GROUPS):
             group_arrived(recv_c, 2, g)
             span = slice(g * height, (g + 1) * height)
-            grads = recv_c[span]
+            grads = unpack(recv_c[span])
             for j in range(ffh // part):
                 lo = j * part
                 hg = dot_t(grads, w_o[0, 0, lo : lo + part, :])
                 joined[span, lo : lo + part] = (hg * gate_f[span, lo : lo + part]).astype(BF)
                 joined[span, ffh + lo : ffh + lo + part] = (hg * up_f[span, lo : lo + part]).astype(BF)
-            send_d[span] = dot_t(joined[span], w_gu[0, 0]).astype(BF)
+            send_d[span] = pack(dot_t(joined[span], w_gu[0, 0]))
             give_back(send_d, recv_d, 3, g)
 
         arrived(recv_d, 3)
-        back = recv_d[...]
+        back = unpack(recv_d[...])
         lg = (dot(take0[...], back) + dot(take1[...], back)).astype(BF)
         inv = inv_f[:, 0:1]
         dotted = jnp.sum(lg.astype(F32) * lat_f[...], axis=1, keepdims=True) / width
@@ -540,7 +564,7 @@
     slots = experts * SLOT
     vm = pltpu.VMEM
     dma = pltpu.SemaphoreType.DMA
-    rows = [vm((slots, lat_w), BF) for _ in range(8)]
+    rows = [vm((slots, 3 * lat_w // 4), BF) for _ in range(8)]
     spec = pl.BlockSpec(memory_space=pltpu.VMEM)
     shape = jax.ShapeDtypeStruct((1, toks, width), BF)
     return pl.pallas_call(

time: 201 us -> 191 us (0.950)
  Pallas kernels: 196 us -> 186 us
    pallas_call x1, Pallas kernels: 196 us -> 186 us  [body(): pl.pallas_call(functools.partial(kernel, sections, experts), out_shape=(s...]
where the time goes in v5:
time: 191 us
  Pallas kernels  186 us (97%)
  local copies, waits for them, and re-layouts  3.35 us (2%)
    pallas_call x1, Pallas kernels, body(): pl.pallas_call(functools.partial(kernel, sections, experts), out_shape=(s...  186 us

profile of v5, /device:TPU:1, one launch (start us, length us, event | category | flops | bytes accessed | tf_op | source)
XLA Modules:
  0.0 191.0 jit_solution(4929209263584895588)
XLA Ops:
  1.3 186.4 %shard_map.104 = (bf16[1,128,4096]{2,1,0:T(8,128)(2,1)}, bf16[1,128,4096]{2,1,0:T(8,128)(2,1)}) custom-call(bf16[128,4096]{1,0:T(8,128)(2,1)} %tokens.1, bf16[128,4096]{1,0:T(8,128)(2,1)} %cot.1, bf16[1,128,512]{2,1,0:T(8,128)(2,1)} %w_down.1, bf16[1,16,4096]{2,1,0:T(8,128)(2,1)} %w_up.1, bf16[1,1,512,2048]{3,2,1,0:T(8,128)(2,1)} %w_gu.1, ...), custom_call_target="tpu_custom_call" | custom-call | tf_op jit(solution)/shard_map/pallas_call | solution.py:570
  187.7 0.0 copy-start
  187.7 2.4 %copy.14 = bf16[1,128,4096]{2,1,0:T(8,128)(2,1)} copy(bf16[1,128,4096]{2,1,0:T(8,128)(2,1)} %get-tuple-element.4) | data formatting | bytes 2097152
  190.1 0.0 copy-done
  190.1 1.0 copy.15
Async XLA Ops:
  187.7 2.4 %copy-start = (bf16[1,128,4096]{2,1,0:T(8,128)(2,1)S(1)}, bf16[1,128,4096]{2,1,0:T(8,128)(2,1)}, u32[]{:S(2)}) copy-start(bf16[1,128,4096]{2,1,0:T(8,128)(2,1)} %get-tuple-element.5) | copy-start | bytes 3145732

commit v6 on v5

--- a/solution.py
+++ b/solution.py
@@ -12,8 +12,8 @@
 BF = jnp.bfloat16
 F32 = jnp.float32
 SLOT = 16
-GROUPS = 2
-PER = 32 // GROUPS
+CUTS = (0, 11, 22, 32)
+GROUPS = len(CUTS) - 1
 ORDER = sorted(
     [(dx, dy, dc) for dx in range(4) for dy in range(4) for dc in range(2) if (dx, dy, dc) != (0, 0, 0)],
     key=lambda k: -(min(k[0], 4 - k[0]) + min(k[1], 4 - k[1])),
@@ -54,8 +54,9 @@
 
 def kernel(
     sections, experts,
-    tokens, cot, w_down, w_up, w_gu, w_o, routes, gates, counts,
-    out, gin,
+    tokens_hbm, cot_hbm, w_down, w_up, w_gu_hbm, w_o_hbm, routes, gates, counts,
+    out_hbm, gin_hbm,
+    cot, w_gu, w_o, out, gin, ins, outs,
     up_all, down_full, quarter, lat_q,
     x_in, g_in,
     gate_f, up_f, hidden, joined,
@@ -72,9 +73,9 @@
     c = e % 2
     above = (t + 1) % sections
     below = (t + sections - 1) % sections
-    toks, width = tokens.shape
+    toks, width = tokens_hbm.shape
     lat_w = w_down.shape[2]
-    ffh = w_o.shape[2]
+    ffh = w_o_hbm.shape[2]
     last = sections - 1
 
     def at(xx, yy, cc):
@@ -94,6 +95,13 @@
             return carry
 
         lax.fori_loop(0, n, step, 0)
+
+    loads = [
+        pltpu.make_async_copy(src, dst, ins.at[k])
+        for k, (src, dst) in enumerate(((tokens_hbm, x_in), (w_gu_hbm, w_gu), (w_o_hbm, w_o), (cot_hbm, cot)))
+    ]
+    for load in loads:
+        load.start()
 
     barrier = pltpu.get_barrier_semaphore()
 
@@ -197,12 +205,6 @@
     @pl.when(t == 1)
     def _():
         gather_first()
-
-    x_in[...] = tokens[...]
-
-    @pl.when(t == last)
-    def _():
-        g_in[...] = cot[...]
 
     count = counts[...]
     expert_lane = lax.broadcasted_iota(jnp.int32, (toks, experts), 1)
@@ -258,15 +260,16 @@
     def inv_rms(square):
         return lax.rsqrt(square / width + EPS)
 
+    loads[0].wait()
     square = jnp.zeros((toks, 1), F32)
     for j in range(n_chunks):
-        wide = tokens[:, cols_of(j)].astype(F32)
+        wide = x_in[:, cols_of(j)].astype(F32)
         square += jnp.sum(wide * wide, axis=1, keepdims=True)
     inv_f[...] = jnp.broadcast_to(inv_rms(square), inv_f.shape)
     def raw_piece(k):
         total = jnp.zeros((toks, lanes), F32)
         for j in range(n_chunks):
-            total += dot(tokens[:, cols_of(j)], down_chunk(quarter.at[k], j))
+            total += dot(x_in[:, cols_of(j)], down_chunk(quarter.at[k], j))
         return (total * inv_f[...]).astype(BF)
 
     @pl.when(t != 1)
@@ -299,25 +302,29 @@
         loop(t, lambda i: fourth(*up(i)))
         product(t - 1)
 
+    for load in loads[1:]:
+        load.wait()
+
     def block(i):
         return pl.ds(pl.multiple_of(i * SLOT, SLOT), SLOT)
 
     def dispatch(src, dst, k):
         for pos, (dx, dy, dc) in enumerate(ORDER):
             p = (((x + dx) % 4) * 4 + (y + dy) % 4) * 2 + (c + dc) % 2
-            send(src.at[block(p)], dst.at[block(pos)], as_.at[k], ar.at[k, pos // PER], (t, p))
+            g = sum(pos >= cut for cut in CUTS[1:])
+            send(src.at[block(p)], dst.at[block(pos)], as_.at[k], ar.at[k, g], (t, p))
         dst[block(experts - 1)] = src[block(e)]
 
     def give_back(src, dst, k, g):
         for pos, (dx, dy, dc) in enumerate(ORDER):
-            if pos // PER == g:
+            if CUTS[g] <= pos < CUTS[g + 1]:
                 p = (((x + 4 - dx) % 4) * 4 + (y + 4 - dy) % 4) * 2 + (c + dc) % 2
                 send(src.at[block(pos)], dst.at[block(e)], as_.at[k], ar.at[k, 0], (t, p))
         if g == GROUPS - 1:
             dst[block(e)] = src[block(experts - 1)]
 
     def group_arrived(buf, k, g):
-        size = PER if g < GROUPS - 1 else PER - 1
+        size = CUTS[g + 1] - CUTS[g] - (g == GROUPS - 1)
         wait(buf.at[pl.ds(0, size * SLOT)], ar.at[k, g])
 
     def arrived(buf, k):
@@ -337,6 +344,7 @@
 
     @pl.when(t == last)
     def _():
+        g_in[...] = cot[...]
         wait(q_in.at[t], qr.at[t])
         route_grads()
 
@@ -393,10 +401,9 @@
         q_in[t - 1] = back_through(cot, t - 1).astype(BF)
 
     part = 256
-    height = PER * SLOT
     for g in range(GROUPS):
         group_arrived(recv_a, 0, g)
-        span = slice(g * height, (g + 1) * height)
+        span = slice(CUTS[g] * SLOT, CUTS[g + 1] * SLOT)
         rows = unpack(recv_a[span])
         for j in range(ffh // part):
             lo = j * part
@@ -413,6 +420,8 @@
         def _():
             give_back(send_b, recv_b, 1, g)
 
+    store_out = pltpu.make_async_copy(out, out_hbm, outs.at[0])
+
     def forward_finish():
         @pl.when(t == last)
         def _():
@@ -442,6 +451,7 @@
         for j in range(n_chunks):
             new = x_in[:, cols_of(j)].astype(F32) + dot(mixed_out[...], up_chunk(t, j))
             out[0, :, cols_of(j)] = new.astype(BF)
+        store_out.start()
 
         @pl.when(t == 0)
         def _():
@@ -459,7 +469,7 @@
 
         for g in range(GROUPS):
             group_arrived(recv_c, 2, g)
-            span = slice(g * height, (g + 1) * height)
+            span = slice(CUTS[g] * SLOT, CUTS[g + 1] * SLOT)
             grads = unpack(recv_c[span])
             for j in range(ffh // part):
                 lo = j * part
@@ -514,6 +524,8 @@
             def _():
                 send(gin.at[0, :, here], g_in.at[:, here], gs.at[j], gr.at[j], (below, e))
 
+            pltpu.make_async_copy(gin.at[:, :, here], gin_hbm.at[:, :, here], outs.at[1 + j]).start()
+
     def stage(i):
         @pl.when((i == 0) == (t == last))
         def _():
@@ -524,6 +536,11 @@
             forward_finish()
 
     loop(2, stage)
+
+    store_out.wait()
+    for j in range(4):
+        here = pl.ds(j * wide_chunk, wide_chunk)
+        pltpu.make_async_copy(gin.at[:, :, here], gin_hbm.at[:, :, here], outs.at[1 + j]).wait()
 
     @pl.when(t == 0)
     def _():
@@ -555,6 +572,28 @@
         loop(t, lambda i: wait(mixed_out, qs.at[i]))
         for j in range(4):
             wait(g_in.at[:, pl.ds(0, wide_chunk)], gs.at[j])
+
+
+def hand_over(out, gin, out_to, gin_to, held, loads, stores):
+    rows = out.shape[1] // 4
+    ways = []
+    for k in range(8):
+        src, dst = ((out, out_to), (gin, gin_to))[k // 4]
+        part = pl.ds((k % 4) * rows, rows)
+        slot = held.at[k // 4, :, part]
+        ways.append(
+            (
+                pltpu.make_async_copy(src.at[:, part], slot, loads.at[k]),
+                pltpu.make_async_copy(slot, dst.at[:, part], stores.at[k]),
+            )
+        )
+    for load, _ in ways:
+        load.start()
+    for load, store in ways:
+        load.wait()
+        store.start()
+    for _, store in ways:
+        store.wait()
 
 
 def body(sections, experts, tokens, cot, w_down, w_up, w_gu, w_o, routes, gates, counts):
@@ -567,12 +606,19 @@
     rows = [vm((slots, 3 * lat_w // 4), BF) for _ in range(8)]
     spec = pl.BlockSpec(memory_space=pltpu.VMEM)
     shape = jax.ShapeDtypeStruct((1, toks, width), BF)
-    return pl.pallas_call(
+    hbm = pl.BlockSpec(memory_space=pl.ANY)
+    results = pl.pallas_call(
         functools.partial(kernel, sections, experts),
         out_shape=(shape, shape),
-        in_specs=[spec] * 9,
-        out_specs=(spec, spec),
+        in_specs=[hbm, hbm, spec, spec, hbm, hbm, spec, spec, spec],
+        out_specs=(hbm, hbm),
         scratch_shapes=[
+            vm((toks, width), BF),
+            vm(w_gu.shape, BF),
+            vm(w_o.shape, BF),
+            vm((1, toks, width), BF),
+            vm((1, toks, width), BF),
+            dma((4,)), dma((5,)),
             vm((sections, 4, 4, 2, lat_w // experts, width), BF),
             vm((4, 4, 2, width // experts, lat_w), BF),
             vm((2, 4, 4, 2, width // experts, lat_w // sections), BF),
@@ -611,6 +657,14 @@
     )(
         tokens, cot, w_down, w_up, w_gu, w_o, jnp.swapaxes(routes, 1, 2), jnp.swapaxes(gates, 1, 2), counts
     )
+    return pl.pallas_call(
+        hand_over,
+        out_shape=(shape, shape),
+        in_specs=[hbm, hbm],
+        out_specs=(hbm, hbm),
+        scratch_shapes=[vm((2, 1, toks, width), BF), dma((8,)), dma((8,))],
+        compiler_params=pltpu.CompilerParams(vmem_limit_bytes=60 * 1024 * 1024),
+    )(*results)
 
 
 def solution(mesh):

time: 191 us -> 188 us (0.984)
  local copies, waits for them, and re-layouts: 3.35 us -> 0 us
    unnamed x4 -> x0, local copies, waits for them, and re-layouts: 3.35 us -> none
    pallas_call x1, Pallas kernels: 186 us -> 184 us  [body(): pl.pallas_call(functools.partial(kernel, sections, experts), out_shape=(s...]
    pallas_call x0 -> x1, Pallas kernels: none -> 2.4 us  [body(): pl.pallas_call(hand_over, out_shape=(shape, shape), in_specs=[hbm, hbm],...]
where the time goes in v6:
time: 188 us
  Pallas kernels  186 us (99%)
    pallas_call x1, Pallas kernels, body(): pl.pallas_call(functools.partial(kernel, sections, experts), out_shape=(s...  184 us

profile of v6, /device:TPU:1, one launch (start us, length us, event | category | flops | bytes accessed | tf_op | source)
XLA Modules:
  0.0 187.6 jit_solution(3404599006013387144)
XLA Ops:
  1.3 183.8 %shard_map.104 = (bf16[1,128,4096]{2,1,0:T(8,128)(2,1)}, bf16[1,128,4096]{2,1,0:T(8,128)(2,1)}) custom-call(bf16[128,4096]{1,0:T(8,128)(2,1)} %tokens_hbm.1, bf16[128,4096]{1,0:T(8,128)(2,1)} %cot_hbm.1, bf16[1,128,512]{2,1,0:T(8,128)(2,1)} %w_down.1, bf16[1,16,4096]{2,1,0:T(8,128)(2,1)} %w_up.1, bf16[1,1,512,2048]{3,2,1,0:T(8,128)(2,1)} %w_gu_hbm.1, ...), custom_call_target="tpu_custom_call" | custom-call | tf_op jit(solution)/shard_map/pallas_call | solution.py:610
  185.0 2.4 %shard_map.105 = (bf16[1,128,4096]{2,1,0:T(8,128)(2,1)}, bf16[1,128,4096]{2,1,0:T(8,128)(2,1)}) custom-call(bf16[1,128,4096]{2,1,0:T(8,128)(2,1)} %get-tuple-element.4.out, bf16[1,128,4096]{2,1,0:T(8,128)(2,1)} %get-tuple-element.5.gin), custom_call_target="tpu_custom_call" | custom-call | tf_op jit(solution)/shard_map/pallas_call | solution.py:660

commit v7 on v6

--- a/solution.py
+++ b/solution.py
@@ -56,7 +56,7 @@
     sections, experts,
     tokens_hbm, cot_hbm, w_down, w_up, w_gu_hbm, w_o_hbm, routes, gates, counts,
     out_hbm, gin_hbm,
-    cot, w_gu, w_o, out, gin, ins, outs,
+    cot, w_gu, w_o, w_gu_t, w_o_t, out, gin, ins, outs,
     up_all, down_full, quarter, lat_q,
     x_in, g_in,
     gate_f, up_f, hidden, joined,
@@ -160,19 +160,22 @@
         )
 
     down = (down_full, d_a, d_b, ds, dr)
-    piece = (quarter.at[0], d_a, d_b, fs.at[0], fr.at[0])
-    piece2 = (quarter.at[1], d_a, d_b, fs.at[1], fr.at[1])
+
+    def piece(k):
+        return (quarter.at[k], d_a, d_b, fs.at[k], fr.at[k])
+
+    own_pieces = sections - 1
+    ends = (t == 0) | (t == last)
 
     lanes = lat_w // sections
 
     @pl.when(t == 0)
     def _():
-        for k in range(2, sections):
-            send(w_down.at[0, :, pl.ds(k * lanes, lanes)], quarter.at[0, x, y, c], zs.at[0], zr.at[0], (k, e))
-        quarter[0, x, y, c] = w_down[0, :, 0:lanes]
-        quarter[1, x, y, c] = w_down[0, :, lanes : 2 * lanes]
-        first(*piece)
-        first(*piece2)
+        there = w_down.at[0, :, pl.ds(own_pieces * lanes, lanes)]
+        send(there, quarter.at[0, x, y, c], zs.at[0], zr.at[0], (last, e))
+        for k in range(own_pieces):
+            quarter[k, x, y, c] = w_down[0, :, k * lanes : (k + 1) * lanes]
+            first(*piece(k))
 
     up_all[t, x, y, c] = w_up[0]
     for k in range(1, sections):
@@ -185,10 +188,10 @@
     def _():
         send(w_up.at[0], up_all.at[t, x, y, c], zs.at[1], zr.at[1 + t], (0, e))
 
-    @pl.when(t > 1)
+    @pl.when(t == last)
     def _():
         wait(quarter.at[0, 0, 0, 0], zr.at[0])
-        first(*piece)
+        first(*piece(0))
 
     def product(i):
         m_all[i] = dot(up_all[i].reshape(lat_w, width), down_full[...].reshape(width, lat_w)).astype(BF)
@@ -202,7 +205,7 @@
             wait(w_up.at[0], zr.at[1 + i])
             first(*up(i))
 
-    @pl.when(t == 1)
+    @pl.when((t > 0) & (t < last))
     def _():
         gather_first()
 
@@ -237,13 +240,17 @@
     gate0 = column(gates[0, 0:1])[:, 0:1]
     gate1 = column(gates[0, 1:2])[:, 0:1]
 
-    @pl.when(t != 1)
-    def _():
-        second(*piece)
-
-    @pl.when(t == 0)
-    def _():
-        second(*piece2)
+    def extra(fn):
+        @pl.when(t == 0)
+        def _():
+            for k in range(1, own_pieces):
+                fn(k)
+
+    @pl.when(ends)
+    def _():
+        second(*piece(0))
+
+    extra(lambda k: second(*piece(k)))
 
     chunk = 512
     n_chunks = width // chunk
@@ -272,22 +279,24 @@
             total += dot(x_in[:, cols_of(j)], down_chunk(quarter.at[k], j))
         return (total * inv_f[...]).astype(BF)
 
-    @pl.when(t != 1)
-    def _():
-        third(*piece)
+    @pl.when(ends)
+    def _():
+        third(*piece(0))
+
+    extra(lambda k: third(*piece(k)))
+
+    @pl.when(ends)
+    def _():
+        fourth(*piece(0))
+        lat_q[t] = raw_piece(0)
 
     @pl.when(t == 0)
     def _():
-        third(*piece2)
-        fourth(*piece2)
-        lat_q[1] = raw_piece(1)
-
-    @pl.when(t != 1)
-    def _():
-        fourth(*piece)
-        lat_q[t] = raw_piece(0)
-
-    @pl.when(t > 1)
+        for k in range(1, own_pieces):
+            fourth(*piece(k))
+            lat_q[k] = raw_piece(k)
+
+    @pl.when(t == last)
     def _():
         send(lat_q.at[t], lat_q.at[t], zs.at[2], zr.at[5], (0, e))
         gather_first()
@@ -304,6 +313,16 @@
 
     for load in loads[1:]:
         load.wait()
+
+    def turn_weights():
+        for j in range(ffh // 256):
+            w_o_t[:, j * 256 : (j + 1) * 256] = w_o[0, 0, j * 256 : (j + 1) * 256, :].T
+        for j in range(2 * ffh // 256):
+            w_gu_t[j * 256 : (j + 1) * 256, :] = w_gu[0, 0, :, j * 256 : (j + 1) * 256].T
+
+    @pl.when(t == last)
+    def _():
+        turn_weights()
 
     def block(i):
         return pl.ds(pl.multiple_of(i * SLOT, SLOT), SLOT)
@@ -377,7 +396,7 @@
 
     @pl.when(t == 0)
     def _():
-        wait(lat_q.at[pl.ds(0, sections - 2)], zr.at[5])
+        wait(lat_q.at[last], zr.at[5])
         lat_f[...] = jnp.concatenate([lat_q[k] for k in range(sections)], axis=1).astype(F32)
 
     @pl.when(t > 0)
@@ -453,6 +472,10 @@
             out[0, :, cols_of(j)] = new.astype(BF)
         store_out.start()
 
+        @pl.when(t < last)
+        def _():
+            turn_weights()
+
         @pl.when(t == 0)
         def _():
             down_full[x, y, c] = w_down[0]
@@ -473,10 +496,10 @@
             grads = unpack(recv_c[span])
             for j in range(ffh // part):
                 lo = j * part
-                hg = dot_t(grads, w_o[0, 0, lo : lo + part, :])
+                hg = dot(grads, w_o_t[:, lo : lo + part])
                 joined[span, lo : lo + part] = (hg * gate_f[span, lo : lo + part]).astype(BF)
                 joined[span, ffh + lo : ffh + lo + part] = (hg * up_f[span, lo : lo + part]).astype(BF)
-            send_d[span] = pack(dot_t(joined[span], w_gu[0, 0]))
+            send_d[span] = pack(dot(joined[span], w_gu_t[...]))
             give_back(send_d, recv_d, 3, g)
 
         arrived(recv_d, 3)
@@ -544,18 +567,19 @@
 
     @pl.when(t == 0)
     def _():
-        wait(lat_q.at[pl.ds(0, sections - 2)], zs.at[0])
-        gather_done(*piece2)
+        wait(lat_q.at[0], zs.at[0])
         gather_done(*up(last))
         wait(q_out.at[0], qs.at[0])
 
-    @pl.when(t > 1)
+    @pl.when(t == last)
     def _():
         wait(lat_q.at[0], zs.at[2])
 
-    @pl.when(t != 1)
-    def _():
-        gather_done(*piece)
+    @pl.when(ends)
+    def _():
+        gather_done(*piece(0))
+
+    extra(lambda k: gather_done(*piece(k)))
 
     loop(jnp.where(t == last, 1, last - t), lambda i: wait(w_up.at[0], zs.at[1]))
     gather_done(*down)
@@ -616,12 +640,14 @@
             vm((toks, width), BF),
             vm(w_gu.shape, BF),
             vm(w_o.shape, BF),
+            vm((2 * ffh, lat_w), BF),
+            vm((lat_w, ffh), BF),
             vm((1, toks, width), BF),
             vm((1, toks, width), BF),
             dma((4,)), dma((5,)),
             vm((sections, 4, 4, 2, lat_w // experts, width), BF),
             vm((4, 4, 2, width // experts, lat_w), BF),
-            vm((2, 4, 4, 2, width // experts, lat_w // sections), BF),
+            vm((sections - 1, 4, 4, 2, width // experts, lat_w // sections), BF),
             vm((sections, toks, lat_w // sections), BF),
             vm((toks, width), BF),
             vm((toks, width), BF),
@@ -645,7 +671,7 @@
             dma((4,)), dma((7,)),
             dma((sections, 5)), dma((sections, 5)),
             dma((5,)), dma((5,)),
-            dma((2, 5)), dma((2, 5)),
+            dma((sections - 1, 5)), dma((sections - 1, 5)),
             dma((4,)), dma((4, GROUPS)),
             dma((sections,)), dma((sections,)),
             dma((sections,)), dma((sections,)),

time: 188 us -> 185 us (0.984)
  Pallas kernels: 186 us -> 183 us
    pallas_call x1, Pallas kernels: 184 us -> 181 us  [body(): pl.pallas_call(functools.partial(kernel, sections, experts), out_shape=(s...]
where the time goes in v7:
time: 185 us
  Pallas kernels  183 us (99%)
    pallas_call x1, Pallas kernels, body(): pl.pallas_call(functools.partial(kernel, sections, experts), out_shape=(s...  181 us

profile of v7, /device:TPU:1, one launch (start us, length us, event | category | flops | bytes accessed | tf_op | source)
XLA Modules:
  0.0 184.7 jit_solution(14547087674242446295)
XLA Ops:
  1.3 180.9 %shard_map.104 = (bf16[1,128,4096]{2,1,0:T(8,128)(2,1)}, bf16[1,128,4096]{2,1,0:T(8,128)(2,1)}) custom-call(bf16[128,4096]{1,0:T(8,128)(2,1)} %tokens_hbm.1, bf16[128,4096]{1,0:T(8,128)(2,1)} %cot_hbm.1, bf16[1,128,512]{2,1,0:T(8,128)(2,1)} %w_down.1, bf16[1,16,4096]{2,1,0:T(8,128)(2,1)} %w_up.1, bf16[1,1,512,2048]{3,2,1,0:T(8,128)(2,1)} %w_gu_hbm.1, ...), custom_call_target="tpu_custom_call" | custom-call | tf_op jit(solution)/shard_map/pallas_call | solution.py:634
  182.2 2.4 %shard_map.105 = (bf16[1,128,4096]{2,1,0:T(8,128)(2,1)}, bf16[1,128,4096]{2,1,0:T(8,128)(2,1)}) custom-call(bf16[1,128,4096]{2,1,0:T(8,128)(2,1)} %get-tuple-element.4.out, bf16[1,128,4096]{2,1,0:T(8,128)(2,1)} %get-tuple-element.5.gin), custom_call_target="tpu_custom_call" | custom-call | tf_op jit(solution)/shard_map/pallas_call | solution.py:686

commit v8 on v7

--- a/solution.py
+++ b/solution.py
@@ -111,103 +111,6 @@
 
     for k in range(1, sections):
         pl.semaphore_signal(barrier, inc=1, device_id=((t + k) % sections, e), device_id_type=MESH)
-    pl.semaphore_wait(barrier, experts - 1 + sections - 1)
-
-    def first(buf, ha, hb, ss, rs):
-        for d in range(1, 4):
-            blk = buf.at[(x, y, c) + ha]
-            send(blk, blk, ss.at[0], rs.at[0], at((x + d) % 4, y, c))
-            blk = buf.at[(x, y, c) + hb]
-            send(blk, blk, ss.at[1], rs.at[1], at(x, (y + d) % 4, c))
-
-    def second(buf, ha, hb, ss, rs):
-        wait(buf.at[(pl.ds(0, 3), 0, 0) + ha], rs.at[0])
-        wait(buf.at[(pl.ds(0, 3), 0, 0) + hb], rs.at[1])
-        for d in range(1, 4):
-            blk = buf.at[(slice(None), y, c) + ha]
-            send(blk, blk, ss.at[2], rs.at[2], at(x, (y + d) % 4, c))
-            blk = buf.at[(x, slice(None), c) + hb]
-            send(blk, blk, ss.at[3], rs.at[3], at((x + d) % 4, y, c))
-
-    def third(buf, ha, hb, ss, rs):
-        wait(buf.at[(pl.ds(0, 3), slice(None), 0) + ha], rs.at[2])
-        wait(buf.at[(pl.ds(0, 3), slice(None), 0) + hb], rs.at[3])
-        blk = buf.at[:, :, c]
-        send(blk, blk, ss.at[4], rs.at[4], at(x, y, 1 - c))
-
-    def fourth(buf, ha, hb, ss, rs):
-        wait(buf.at[:, :, 0], rs.at[4])
-
-    def gather_done(buf, ha, hb, ss, rs):
-        wait(buf.at[(pl.ds(0, 3), 0, 0) + ha], ss.at[0])
-        wait(buf.at[(pl.ds(0, 3), 0, 0) + hb], ss.at[1])
-        wait(buf.at[(pl.ds(0, 3), slice(None), 0) + ha], ss.at[2])
-        wait(buf.at[(pl.ds(0, 3), slice(None), 0) + hb], ss.at[3])
-        wait(buf.at[:, :, 0], ss.at[4])
-
-    half_cols = width // 2
-    half_rows = w_down.shape[1] // 2
-    d_a = (pl.ds(0, half_rows), slice(None))
-    d_b = (pl.ds(half_rows, half_rows), slice(None))
-
-    def up(i):
-        return (
-            up_all.at[i],
-            (slice(None), pl.ds(0, half_cols)),
-            (slice(None), pl.ds(half_cols, half_cols)),
-            us.at[i],
-            ur.at[i],
-        )
-
-    down = (down_full, d_a, d_b, ds, dr)
-
-    def piece(k):
-        return (quarter.at[k], d_a, d_b, fs.at[k], fr.at[k])
-
-    own_pieces = sections - 1
-    ends = (t == 0) | (t == last)
-
-    lanes = lat_w // sections
-
-    @pl.when(t == 0)
-    def _():
-        there = w_down.at[0, :, pl.ds(own_pieces * lanes, lanes)]
-        send(there, quarter.at[0, x, y, c], zs.at[0], zr.at[0], (last, e))
-        for k in range(own_pieces):
-            quarter[k, x, y, c] = w_down[0, :, k * lanes : (k + 1) * lanes]
-            first(*piece(k))
-
-    up_all[t, x, y, c] = w_up[0]
-    for k in range(1, sections):
-
-        @pl.when(t < k)
-        def _():
-            send(w_up.at[0], up_all.at[t, x, y, c], zs.at[1], zr.at[1 + t], (k, e))
-
-    @pl.when(t == last)
-    def _():
-        send(w_up.at[0], up_all.at[t, x, y, c], zs.at[1], zr.at[1 + t], (0, e))
-
-    @pl.when(t == last)
-    def _():
-        wait(quarter.at[0, 0, 0, 0], zr.at[0])
-        first(*piece(0))
-
-    def product(i):
-        m_all[i] = dot(up_all[i].reshape(lat_w, width), down_full[...].reshape(width, lat_w)).astype(BF)
-
-    def gather_first():
-        down_full[x, y, c] = w_down[0]
-        first(*down)
-
-        @functools.partial(loop, t)
-        def _(i):
-            wait(w_up.at[0], zr.at[1 + i])
-            first(*up(i))
-
-    @pl.when((t > 0) & (t < last))
-    def _():
-        gather_first()
 
     count = counts[...]
     expert_lane = lax.broadcasted_iota(jnp.int32, (toks, experts), 1)
@@ -240,29 +143,11 @@
     gate0 = column(gates[0, 0:1])[:, 0:1]
     gate1 = column(gates[0, 1:2])[:, 0:1]
 
-    def extra(fn):
-        @pl.when(t == 0)
-        def _():
-            for k in range(1, own_pieces):
-                fn(k)
-
-    @pl.when(ends)
-    def _():
-        second(*piece(0))
-
-    extra(lambda k: second(*piece(k)))
-
     chunk = 512
     n_chunks = width // chunk
 
     def cols_of(j):
         return slice(j * chunk, (j + 1) * chunk)
-
-    def up_chunk(i, j):
-        return up_all[i, :, :, :, :, j * chunk : (j + 1) * chunk].reshape(lat_w, chunk)
-
-    def down_chunk(buf, j):
-        return buf[j // 2, 2 * (j % 2) : 2 * (j % 2) + 2].reshape(chunk, buf.shape[-1])
 
     def inv_rms(square):
         return lax.rsqrt(square / width + EPS)
@@ -273,6 +158,126 @@
         wide = x_in[:, cols_of(j)].astype(F32)
         square += jnp.sum(wide * wide, axis=1, keepdims=True)
     inv_f[...] = jnp.broadcast_to(inv_rms(square), inv_f.shape)
+    pl.semaphore_wait(barrier, experts - 1 + sections - 1)
+
+    def first(buf, ha, hb, ss, rs):
+        for d in range(1, 4):
+            blk = buf.at[(x, y, c) + ha]
+            send(blk, blk, ss.at[0], rs.at[0], at((x + d) % 4, y, c))
+            blk = buf.at[(x, y, c) + hb]
+            send(blk, blk, ss.at[1], rs.at[1], at(x, (y + d) % 4, c))
+
+    def second(buf, ha, hb, ss, rs):
+        wait(buf.at[(pl.ds(0, 3), 0, 0) + ha], rs.at[0])
+        wait(buf.at[(pl.ds(0, 3), 0, 0) + hb], rs.at[1])
+        for d in range(1, 4):
+            blk = buf.at[(slice(None), y, c) + ha]
+            send(blk, blk, ss.at[2], rs.at[2], at(x, (y + d) % 4, c))
+            blk = buf.at[(x, slice(None), c) + hb]
+            send(blk, blk, ss.at[3], rs.at[3], at((x + d) % 4, y, c))
+
+    def third(buf, ha, hb, ss, rs):
+        wait(buf.at[(pl.ds(0, 3), slice(None), 0) + ha], rs.at[2])
+        wait(buf.at[(pl.ds(0, 3), slice(None), 0) + hb], rs.at[3])
+        blk = buf.at[:, :, c]
+        send(blk, blk, ss.at[4], rs.at[4], at(x, y, 1 - c))
+
+    def fourth(buf, ha, hb, ss, rs):
+        wait(buf.at[:, :, 0], rs.at[4])
+
+    def gather_done(buf, ha, hb, ss, rs):
+        wait(buf.at[(pl.ds(0, 3), 0, 0) + ha], ss.at[0])
+        wait(buf.at[(pl.ds(0, 3), 0, 0) + hb], ss.at[1])
+        wait(buf.at[(pl.ds(0, 3), slice(None), 0) + ha], ss.at[2])
+        wait(buf.at[(pl.ds(0, 3), slice(None), 0) + hb], ss.at[3])
+        wait(buf.at[:, :, 0], ss.at[4])
+
+    half_cols = width // 2
+    half_rows = w_down.shape[1] // 2
+    d_a = (pl.ds(0, half_rows), slice(None))
+    d_b = (pl.ds(half_rows, half_rows), slice(None))
+
+    def up(i):
+        return (
+            up_all.at[i],
+            (slice(None), pl.ds(0, half_cols)),
+            (slice(None), pl.ds(half_cols, half_cols)),
+            us.at[i],
+            ur.at[i],
+        )
+
+    down = (down_full, d_a, d_b, ds, dr)
+
+    def piece(k):
+        return (quarter.at[k], d_a, d_b, fs.at[k], fr.at[k])
+
+    own_pieces = sections - 1
+    ends = (t == 0) | (t == last)
+
+    lanes = lat_w // sections
+
+    @pl.when(t == 0)
+    def _():
+        there = w_down.at[0, :, pl.ds(own_pieces * lanes, lanes)]
+        send(there, quarter.at[0, x, y, c], zs.at[0], zr.at[0], (last, e))
+        for k in range(own_pieces):
+            quarter[k, x, y, c] = w_down[0, :, k * lanes : (k + 1) * lanes]
+            first(*piece(k))
+
+    up_all[t, x, y, c] = w_up[0]
+    for k in range(1, sections):
+
+        @pl.when(t < k)
+        def _():
+            send(w_up.at[0], up_all.at[t, x, y, c], zs.at[1], zr.at[1 + t], (k, e))
+
+    @pl.when(t == last)
+    def _():
+        send(w_up.at[0], up_all.at[t, x, y, c], zs.at[1], zr.at[1 + t], (0, e))
+
+    @pl.when(t == last)
+    def _():
+        wait(quarter.at[0, 0, 0, 0], zr.at[0])
+        first(*piece(0))
+
+    def product(i):
+        m_all[i] = dot(up_all[i].reshape(lat_w, width), down_full[...].reshape(width, lat_w)).astype(BF)
+
+    def gather_first():
+        down_full[x, y, c] = w_down[0]
+        first(*down)
+
+        @functools.partial(loop, t)
+        def _(i):
+            wait(w_up.at[0], zr.at[1 + i])
+            first(*up(i))
+
+    @pl.when((t > 0) & (t < last))
+    def _():
+        gather_first()
+
+    def extra(fn):
+        @pl.when(t == 0)
+        def _():
+            for k in range(1, own_pieces):
+                fn(k)
+
+    @pl.when(ends)
+    def _():
+        second(*piece(0))
+
+    extra(lambda k: second(*piece(k)))
+
+    @pl.when(t == last)
+    def _():
+        gather_first()
+
+    def up_chunk(i, j):
+        return up_all[i, :, :, :, :, j * chunk : (j + 1) * chunk].reshape(lat_w, chunk)
+
+    def down_chunk(buf, j):
+        return buf[j // 2, 2 * (j % 2) : 2 * (j % 2) + 2].reshape(chunk, buf.shape[-1])
+
     def raw_piece(k):
         total = jnp.zeros((toks, lanes), F32)
         for j in range(n_chunks):
@@ -299,7 +304,6 @@
     @pl.when(t == last)
     def _():
         send(lat_q.at[t], lat_q.at[t], zs.at[2], zr.at[5], (0, e))
-        gather_first()
 
     @pl.when(t > 0)
     def _():
@@ -482,7 +486,6 @@
             for phase in (first, second, third, fourth):
                 phase(*down)
 
-    wide_chunk = width // 4
 
     def backward():
         @pl.when(t < last)
@@ -531,17 +534,16 @@
 
                 mix_grad(i, back_through(x_in, i))
 
-        for j in range(4):
-            here = pl.ds(j * wide_chunk, wide_chunk)
+        for j in range(n_chunks):
+            here = pl.ds(j * chunk, chunk)
 
             @pl.when(t < last)
             def _():
                 wait(g_in.at[:, here], gr.at[j])
 
-            for h in range(2 * j, 2 * j + 2):
-                ng = dot_t(lg, down_chunk(down_full, h))
-                new = g_in[:, cols_of(h)].astype(F32) + inv * ng - scale * x_in[:, cols_of(h)].astype(F32)
-                gin[0, :, cols_of(h)] = new.astype(BF)
+            ng = dot_t(lg, down_chunk(down_full, j))
+            new = g_in[:, cols_of(j)].astype(F32) + inv * ng - scale * x_in[:, cols_of(j)].astype(F32)
+            gin[0, :, cols_of(j)] = new.astype(BF)
 
             @pl.when(t > 0)
             def _():
@@ -561,8 +563,8 @@
     loop(2, stage)
 
     store_out.wait()
-    for j in range(4):
-        here = pl.ds(j * wide_chunk, wide_chunk)
+    for j in range(n_chunks):
+        here = pl.ds(j * chunk, chunk)
         pltpu.make_async_copy(gin.at[:, :, here], gin_hbm.at[:, :, here], outs.at[1 + j]).wait()
 
     @pl.when(t == 0)
@@ -594,8 +596,8 @@
     @pl.when(t > 0)
     def _():
         loop(t, lambda i: wait(mixed_out, qs.at[i]))
-        for j in range(4):
-            wait(g_in.at[:, pl.ds(0, wide_chunk)], gs.at[j])
+        for j in range(n_chunks):
+            wait(g_in.at[:, pl.ds(0, chunk)], gs.at[j])
 
 
 def hand_over(out, gin, out_to, gin_to, held, loads, stores):
@@ -644,7 +646,7 @@
             vm((lat_w, ffh), BF),
             vm((1, toks, width), BF),
             vm((1, toks, width), BF),
-            dma((4,)), dma((5,)),
+            dma((4,)), dma((9,)),
             vm((sections, 4, 4, 2, lat_w // experts, width), BF),
             vm((4, 4, 2, width // experts, lat_w), BF),
             vm((sections - 1, 4, 4, 2, width // experts, lat_w // sections), BF),
@@ -675,7 +677,7 @@
             dma((4,)), dma((4, GROUPS)),
             dma((sections,)), dma((sections,)),
             dma((sections,)), dma((sections,)),
-            dma((4,)), dma((4,)),
+            dma((8,)), dma((8,)),
         ],
         compiler_params=pltpu.CompilerParams(
             collective_id=0, has_side_effects=True, vmem_limit_bytes=60 * 1024 * 1024

time: 185 us -> 181 us (0.978)
  Pallas kernels: 183 us -> 180 us
    pallas_call x1, Pallas kernels: 181 us -> 177 us  [body(): pl.pallas_call(functools.partial(kernel, sections, experts), out_shape=(s...]
where the time goes in v8:
time: 181 us
  Pallas kernels  180 us (99%)
    pallas_call x1, Pallas kernels, body(): pl.pallas_call(functools.partial(kernel, sections, experts), out_shape=(s...  177 us

profile of v8, /device:TPU:1, one launch (start us, length us, event | category | flops | bytes accessed | tf_op | source)
XLA Modules:
  0.0 181.1 jit_solution(12230757768470618240)
XLA Ops:
  1.3 177.2 %shard_map.104 = (bf16[1,128,4096]{2,1,0:T(8,128)(2,1)}, bf16[1,128,4096]{2,1,0:T(8,128)(2,1)}) custom-call(bf16[128,4096]{1,0:T(8,128)(2,1)} %tokens_hbm.1, bf16[128,4096]{1,0:T(8,128)(2,1)} %cot_hbm.1, bf16[1,128,512]{2,1,0:T(8,128)(2,1)} %w_down.1, bf16[1,16,4096]{2,1,0:T(8,128)(2,1)} %w_up.1, bf16[1,1,512,2048]{3,2,1,0:T(8,128)(2,1)} %w_gu_hbm.1, ...), custom_call_target="tpu_custom_call" | custom-call | tf_op jit(solution)/shard_map/pallas_call | solution.py:636
  178.5 2.4 %shard_map.105 = (bf16[1,128,4096]{2,1,0:T(8,128)(2,1)}, bf16[1,128,4096]{2,1,0:T(8,128)(2,1)}) custom-call(bf16[1,128,4096]{2,1,0:T(8,128)(2,1)} %get-tuple-element.4.out, bf16[1,128,4096]{2,1,0:T(8,128)(2,1)} %get-tuple-element.5.gin), custom_call_target="tpu_custom_call" | custom-call | tf_op jit(solution)/shard_map/pallas_call | solution.py:688
